TPU v7x, 256 devices: a whole 4x4x8 slice. The times are simulated.
256 devices in a mesh: rows: 64 (over z, y, core), dims: 4 (over x).
Axes of the slice: x: 4, y: 4, z: 8, core: 2. Of those that a mesh axis runs over, the one named last changes fastest.
Arguments:
- table: bfloat16 [1, 256, 262144], P(None, 'dims', 'rows'), may hold values from -6 to 6
- accum: float32 [1, 262144], P(None, 'rows'), may hold values from 0.5 to 8
- grad_pooled: bfloat16 [1, 256, 8192], P(None, 'dims', 'rows'), may hold values from -6 to 6
- sample_slot: int32 [1, 64, 64, 160], P(None, 'rows'), may hold values from 0 to 127
- row_slot: int32 [1, 64, 64, 160], P(None, 'rows'), may hold values from 0 to 4095
- weight: int32 [1, 64, 64, 160], P(None, 'rows'), may hold values from 1 to 3
- send_count: int32 [1, 64, 64], P(None, 'rows'), may hold values from 1 to 160, as said below
Outputs:
- pooled: float32 [1, 256, 8192], P(None, 'dims', 'rows')
- new_table: bfloat16 [1, 256, 262144], P(None, 'dims', 'rows')
- new_accum: float32 [1, 262144], P(None, 'rows')
Inputs may be any that keep to these rules, and one draw needn't show every extreme that they name: `send_count`: at most 160 live entries from one row shard to one owner per feature; in every feature one owner receives exactly 160 from every row shard. Slots at or after the count are unused.
All inputs are finite; a program needn't handle non-finite values.
Results may differ from a plain program's by a relative error of at most 0.001.
Values may be sent and summed in bfloat16 or wider, within the bound.
A program may use at most 64 MiB of HBM per device.

v0:
```python
import math

import jax
import jax.numpy as jnp
from jax import lax
from jax.sharding import PartitionSpec as P

D = 256


step_size = 0.3


def in_one_piece(arrays, axis, split_dim, concat_dim, along):
    ends, at = ([], 0)
    for a in arrays[:-1]:
        at += a.shape[along]
        ends.append(at)
    both = jnp.concatenate(arrays, axis=along)
    return tuple(
        jnp.split(
            lax.all_to_all(both, axis, split_axis=split_dim, concat_axis=concat_dim, tiled=True),
            ends,
            axis=along,
        )
    )


def sent_to_all(value, axis):
    copies = jnp.broadcast_to(value, (lax.axis_size(axis), *value.shape))
    return lax.all_to_all(copies, axis, split_axis=0, concat_axis=0, tiled=True)


def of_everyone(value, axis):
    return sent_to_all(value, axis).sum(axis=0)


def shards(table, accum, grad_pooled, sample_slot, row_slot, weight, send_count):
    feat_count, dim_local, row_local = table.shape
    peer_count = lax.axis_size("rows")
    own_samples = grad_pooled.shape[2]
    slot_count = sample_slot.shape[3]
    entry_count = peer_count * slot_count
    block_rows = math.gcd(row_local, 512)
    block_count = row_local // block_rows
    row_index = row_slot.reshape(feat_count, peer_count, slot_count)
    flat_rows = row_index.reshape(feat_count, 1, entry_count)
    live_count = send_count.reshape(feat_count, peer_count)
    slot_iota = lax.broadcasted_iota(jnp.int32, (1, 1, slot_count), 2)
    live_mask = slot_iota < live_count[:, :, None]
    weights = jnp.where(live_mask, weight.reshape(feat_count, peer_count, slot_count), 0)
    flat_weights = weights.reshape(feat_count, 1, entry_count).astype(jnp.bfloat16)
    block_iota = lax.broadcasted_iota(jnp.int32, (1, block_rows, 1), 1)

    def lookup_block(carry, block):
        start = block * block_rows
        table_part = lax.dynamic_slice_in_dim(table, start, block_rows, 2)
        selector = (flat_rows == block_iota + start).astype(jnp.bfloat16)
        return (
            carry
            + jnp.einsum("fdr,fre->fde", table_part, selector, preferred_element_type=jnp.float32),
            None,
        )

    looked_up, _ = lax.scan(
        lookup_block,
        jnp.zeros((feat_count, dim_local, entry_count), jnp.float32),
        jnp.arange(block_count, dtype=jnp.int32),
    )
    picked = looked_up.astype(jnp.bfloat16).reshape(feat_count, dim_local, peer_count, slot_count)
    positions = lax.broadcasted_iota(jnp.int32, (1, 1, 1, own_samples), 3)
    weight_tiles = weights.reshape(feat_count, 1, peer_count, slot_count)
    arrived_rows, arrived_slots, arrived_weights = (
        lax.all_to_all(picked, "rows", split_axis=2, concat_axis=2, tiled=True),
        *in_one_piece((sample_slot, weight_tiles), "rows", 2, 2, 0),
    )
    arrived_local = arrived_slots[:, 0]
    onehot = jnp.where(
        arrived_local[..., None] == positions, arrived_weights[:, 0][..., None], 0
    ).astype(jnp.bfloat16)
    pooled = jnp.einsum("fdnk,fnkj->fdj", arrived_rows, onehot, preferred_element_type=jnp.float32)
    selector = (arrived_local[..., None] == positions).astype(jnp.bfloat16)
    sample_grads = jnp.einsum(
        "fdj,fnkj->fdnk", grad_pooled, selector, preferred_element_type=jnp.float32
    ).astype(jnp.bfloat16)
    entry_values = lax.all_to_all(sample_grads, "rows", split_axis=2, concat_axis=2, tiled=True)
    entry_flat = entry_values.reshape(feat_count, dim_local, entry_count)

    def gradient_block(block):
        start = block * block_rows
        weighted = jnp.where(flat_rows == block_iota + start, flat_weights, 0)
        return jnp.einsum("fde,fre->fdr", entry_flat, weighted, preferred_element_type=jnp.float32)

    grad_blocks = lax.map(gradient_block, jnp.arange(block_count, dtype=jnp.int32))
    row_grad = jnp.moveaxis(grad_blocks, 0, 2).reshape(feat_count, dim_local, row_local)
    squares = jnp.sum(row_grad * row_grad, axis=1)
    norm_total = of_everyone(squares, "dims")
    new_accum = accum + norm_total / D
    new_table = (
        table.astype(jnp.float32) - step_size * row_grad / jnp.sqrt(new_accum)[:, None, :]
    ).astype(jnp.bfloat16)
    return (pooled, new_table, new_accum)


def solution(mesh):
    return jax.shard_map(
        shards,
        mesh=mesh,
        in_specs=(
            P(None, "dims", "rows"),
            P(None, "rows"),
            P(None, "dims", "rows"),
            P(None, "rows", None, None),
            P(None, "rows", None, None),
            P(None, "rows", None, None),
            P(None, "rows", None),
        ),
        out_specs=(P(None, "dims", "rows"), P(None, "dims", "rows"), P(None, "rows")),
        check_vma=False,
    )
```

profile of v0, /device:TPU:8, one launch (start us, length us, event | category | flops | bytes accessed | tf_op | source)
XLA Modules:
  0.0 189.3 jit_solution(15722483261543867529)
XLA Ops:
  3.2 12.1 %all-to-all-start.1 = ((s32[2,1,64,160]{3,0,1,2:T(2,128)}), s32[2,1,64,160]{3,0,1,2:T(2,128)S(1)}, u32[]{:S(2)}, u32[]{:S(2)}) async-start(s32[2,1,64,160]{3,0,1,2:T(2,128)} %copy.43), calls=%async_computation.1 | async-start | bytes 262144 | tf_op jit(solution)/shard_map/all_to_all | solution.py:22
  15.3 1.0 reshape_reshape.3
  16.3 9.0 %all-to-all-done.1 = s32[2,1,64,160]{3,0,1,2:T(2,128)S(1)} async-done(((s32[2,1,64,160]{3,0,1,2:T(2,128)}), s32[2,1,64,160]{3,0,1,2:T(2,128)S(1)}, u32[]{:S(2)}, u32[]{:S(2)}) %all-to-all-start.1) | async-done | bytes 81952 | tf_op jit(solution)/shard_map/all_to_all | solution.py:22
  25.4 4.9 %convert_bitcast_fusion = bf16[1,64,64,160]{3,1,0,2:T(8,128)(2,1)} fusion(s32[64,160]{1,0:T(8,128)S(1)} %bitcast.88, bf16[1,64,128]{2,1,0:T(8,128)(2,1)S(1)} %copy-done), kind=kOutput, calls=%fused_computation.32 | convolution fusion | flops 169738240 | bytes 1368064 | tf_op jit(solution)/shard_map/fdj,fnkj->fdnk/dot_general | solution.py:83
  30.3 5.7 %all-to-all-start.2 = ((bf16[1,64,64,160]{3,1,0,2:T(8,128)(2,1)}), bf16[1,64,64,160]{3,1,0,2:T(8,128)(2,1)S(1)}, u32[]{:S(2)}, u32[]{:S(2)}) async-start(bf16[1,64,64,160]{3,1,0,2:T(8,128)(2,1)} %convert_bitcast_fusion), calls=%async_computation.2 | async-start | bytes 4194304 | tf_op jit(solution)/shard_map/all_to_all | solution.py:86
  36.0 66.4 %while.25 = (s32[]{:T(128)}, f32[1,64,10240]{2,1,0:T(8,128)}, s32[8]{0:T(128)S(1)}, bf16[1,64,4096]{2,1,0:T(8,128)(2,1)}, s32[1,1,10240]{2,1,0:T(1,128)S(1)}, /*...) while((s32[]{:T(128)}, f32[1,64,10240]{2,1,0:T(8,128)}, s32[8]{0:T(128)S(1)}, ...), condition=%wide.region_1.2_spmd.clone, body=%wide.region_0.1_spmd.clone.sunk | while | flops 677642752 | bytes 5353649 | solution.py:65
  37.3 6.2 %fusion.55 = f32[1,64,10240]{2,1,0:T(8,128)} fusion(s32[10240]{0:T(1024)S(1)} %bitcast.97, s32[512]{0:T(512)S(1)} %bitcast.95, f32[1,64,10240]{2,1,0:T(8,128)} %get-tuple-element.266, pred[]{:T(512)S(6)} %compare.3, bf16[1,64,4096]{2,1,0:T(8,128)(2,1)} %get-tuple-element.277, s32[]{:T(128)S(6)} %select_n.60), kind=kOutput, calls=%fused_computation.5.clone.1 | convolution fusion | flops 677642240 | bytes 5351429 | tf_op jit(solution)/shard_map/while/body/eval_jaxpr/fdr,fre->fde/dot_general | solution.py:61
  44.8 7.2 %fusion.55 = f32[1,64,10240]{2,1,0:T(8,128)} fusion(s32[10240]{0:T(1024)S(1)} %bitcast.97, s32[512]{0:T(512)S(1)} %bitcast.95, f32[1,64,10240]{2,1,0:T(8,128)} %get-tuple-element.266, pred[]{:T(512)S(6)} %compare.3, bf16[1,64,4096]{2,1,0:T(8,128)(2,1)} %get-tuple-element.277, s32[]{:T(128)S(6)} %select_n.60), kind=kOutput, calls=%fused_computation.5.clone.1 | convolution fusion | flops 677642240 | bytes 5351429 | tf_op jit(solution)/shard_map/while/body/eval_jaxpr/fdr,fre->fde/dot_general | solution.py:61
  53.2 7.2 %fusion.55 = f32[1,64,10240]{2,1,0:T(8,128)} fusion(s32[10240]{0:T(1024)S(1)} %bitcast.97, s32[512]{0:T(512)S(1)} %bitcast.95, f32[1,64,10240]{2,1,0:T(8,128)} %get-tuple-element.266, pred[]{:T(512)S(6)} %compare.3, bf16[1,64,4096]{2,1,0:T(8,128)(2,1)} %get-tuple-element.277, s32[]{:T(128)S(6)} %select_n.60), kind=kOutput, calls=%fused_computation.5.clone.1 | convolution fusion | flops 677642240 | bytes 5351429 | tf_op jit(solution)/shard_map/while/body/eval_jaxpr/fdr,fre->fde/dot_general | solution.py:61
  61.6 7.2 %fusion.55 = f32[1,64,10240]{2,1,0:T(8,128)} fusion(s32[10240]{0:T(1024)S(1)} %bitcast.97, s32[512]{0:T(512)S(1)} %bitcast.95, f32[1,64,10240]{2,1,0:T(8,128)} %get-tuple-element.266, pred[]{:T(512)S(6)} %compare.3, bf16[1,64,4096]{2,1,0:T(8,128)(2,1)} %get-tuple-element.277, s32[]{:T(128)S(6)} %select_n.60), kind=kOutput, calls=%fused_computation.5.clone.1 | convolution fusion | flops 677642240 | bytes 5351429 | tf_op jit(solution)/shard_map/while/body/eval_jaxpr/fdr,fre->fde/dot_general | solution.py:61
  70.0 7.2 %fusion.55 = f32[1,64,10240]{2,1,0:T(8,128)} fusion(s32[10240]{0:T(1024)S(1)} %bitcast.97, s32[512]{0:T(512)S(1)} %bitcast.95, f32[1,64,10240]{2,1,0:T(8,128)} %get-tuple-element.266, pred[]{:T(512)S(6)} %compare.3, bf16[1,64,4096]{2,1,0:T(8,128)(2,1)} %get-tuple-element.277, s32[]{:T(128)S(6)} %select_n.60), kind=kOutput, calls=%fused_computation.5.clone.1 | convolution fusion | flops 677642240 | bytes 5351429 | tf_op jit(solution)/shard_map/while/body/eval_jaxpr/fdr,fre->fde/dot_general | solution.py:61
  78.4 7.2 %fusion.55 = f32[1,64,10240]{2,1,0:T(8,128)} fusion(s32[10240]{0:T(1024)S(1)} %bitcast.97, s32[512]{0:T(512)S(1)} %bitcast.95, f32[1,64,10240]{2,1,0:T(8,128)} %get-tuple-element.266, pred[]{:T(512)S(6)} %compare.3, bf16[1,64,4096]{2,1,0:T(8,128)(2,1)} %get-tuple-element.277, s32[]{:T(128)S(6)} %select_n.60), kind=kOutput, calls=%fused_computation.5.clone.1 | convolution fusion | flops 677642240 | bytes 5351429 | tf_op jit(solution)/shard_map/while/body/eval_jaxpr/fdr,fre->fde/dot_general | solution.py:61
  86.8 7.2 %fusion.55 = f32[1,64,10240]{2,1,0:T(8,128)} fusion(s32[10240]{0:T(1024)S(1)} %bitcast.97, s32[512]{0:T(512)S(1)} %bitcast.95, f32[1,64,10240]{2,1,0:T(8,128)} %get-tuple-element.266, pred[]{:T(512)S(6)} %compare.3, bf16[1,64,4096]{2,1,0:T(8,128)(2,1)} %get-tuple-element.277, s32[]{:T(128)S(6)} %select_n.60), kind=kOutput, calls=%fused_computation.5.clone.1 | convolution fusion | flops 677642240 | bytes 5351429 | tf_op jit(solution)/shard_map/while/body/eval_jaxpr/fdr,fre->fde/dot_general | solution.py:61
  95.2 7.2 %fusion.55 = f32[1,64,10240]{2,1,0:T(8,128)} fusion(s32[10240]{0:T(1024)S(1)} %bitcast.97, s32[512]{0:T(512)S(1)} %bitcast.95, f32[1,64,10240]{2,1,0:T(8,128)} %get-tuple-element.266, pred[]{:T(512)S(6)} %compare.3, bf16[1,64,4096]{2,1,0:T(8,128)(2,1)} %get-tuple-element.277, s32[]{:T(128)S(6)} %select_n.60), kind=kOutput, calls=%fused_computation.5.clone.1 | convolution fusion | flops 677642240 | bytes 5351429 | tf_op jit(solution)/shard_map/while/body/eval_jaxpr/fdr,fre->fde/dot_general | solution.py:61
  103.1 1.9 convert_element_type.41
  105.0 3.6 %reshape.286 = bf16[1,64,64,160]{3,2,1,0:T(8,128)(2,1)} reshape(bf16[1,64,10240]{2,1,0:T(8,128)(2,1)S(1)} %convert_element_type.41) | data formatting | bytes 2621440 | tf_op jit(solution)/shard_map/reshape | solution.py:70
  108.6 4.1 %copy.42 = bf16[1,64,64,160]{3,1,0,2:T(8,128)(2,1)} copy(bf16[1,64,64,160]{3,2,1,0:T(8,128)(2,1)} %reshape.286) | data formatting | bytes 2621440 | tf_op jit(solution)/shard_map/reshape | solution.py:70
  113.2 10.6 %all-to-all-start = ((bf16[1,64,64,160]{3,1,0,2:T(8,128)(2,1)}), bf16[1,64,64,160]{3,1,0,2:T(8,128)(2,1)}, u32[]{:S(2)}, u32[]{:S(2)}) async-start(bf16[1,64,64,160]{3,1,0,2:T(8,128)(2,1)} %copy.42), calls=%async_computation | async-start | bytes 4194304 | tf_op jit(solution)/shard_map/all_to_all | solution.py:74
  123.8 2.5 %copy.47 = bf16[1,64,64,160]{3,2,1,0:T(8,128)(2,1)} copy(bf16[1,64,64,160]{3,1,0,2:T(8,128)(2,1)S(1)} %all-to-all-done.2) | data formatting | bytes 2621440 | tf_op jit(solution)/shard_map/all_to_all | solution.py:86
  126.3 4.6 %reshape.290 = bf16[1,64,10240]{2,1,0:T(8,128)(2,1)S(1)} reshape(bf16[1,64,64,160]{3,2,1,0:T(8,128)(2,1)} %copy.47) | data formatting | bytes 2621440 | tf_op jit(solution)/shard_map/reshape | solution.py:87
  131.0 38.4 %while.24 = (s32[]{:T(128)}, f32[8,1,64,512]{3,2,1,0:T(8,128)S(1)}, s32[1,1,10240]{2,1,0:T(1,128)S(1)}, s32[8]{0:T(128)S(1)}, bf16[1,1,10240]{2,1,0:T(2,128)(2,1...) while((s32[]{:T(128)}, f32[8,1,64,512]{3,2,1,0:T(8,128)S(1)}, ...), condition=%wide.region_3.4_spmd.clone, body=%wide.region_2.3_spmd.clone.sunk | while | flops 681574912 | bytes 1548423 | solution.py:94
  132.3 3.4 %fusion.52 = f32[8,1,64,512]{3,2,1,0:T(8,128)S(1)} fusion(f32[8,1,64,512]{3,2,1,0:T(8,128)S(1)} %get-tuple-element.293, s32[]{:T(128)S(6)} %copy.68, bf16[1,64,10240]{2,1,0:T(8,128)(2,1)S(1)} %get-tuple-element.306, s32[10240]{0:T(1024)S(1)} %bitcast.98, s32[512]{0:T(512)S(1)} %bitcast.96, bf16[10240]{0:T(1024)(128)(2,1)S(1)} %reduce.6), kind=kOutput, calls=%fused_computation.20.clone.1 | convolution fusion | flops 681574400 | bytes 1505284 | tf_op jit(solution)/shard_map/while/body/eval_jaxpr/fde,fre->fdr/dot_general | solution.py:92
  137.2 3.4 %fusion.52 = f32[8,1,64,512]{3,2,1,0:T(8,128)S(1)} fusion(f32[8,1,64,512]{3,2,1,0:T(8,128)S(1)} %get-tuple-element.293, s32[]{:T(128)S(6)} %copy.68, bf16[1,64,10240]{2,1,0:T(8,128)(2,1)S(1)} %get-tuple-element.306, s32[10240]{0:T(1024)S(1)} %bitcast.98, s32[512]{0:T(512)S(1)} %bitcast.96, bf16[10240]{0:T(1024)(128)(2,1)S(1)} %reduce.6), kind=kOutput, calls=%fused_computation.20.clone.1 | convolution fusion | flops 681574400 | bytes 1505284 | tf_op jit(solution)/shard_map/while/body/eval_jaxpr/fde,fre->fdr/dot_general | solution.py:92
  142.0 3.4 %fusion.52 = f32[8,1,64,512]{3,2,1,0:T(8,128)S(1)} fusion(f32[8,1,64,512]{3,2,1,0:T(8,128)S(1)} %get-tuple-element.293, s32[]{:T(128)S(6)} %copy.68, bf16[1,64,10240]{2,1,0:T(8,128)(2,1)S(1)} %get-tuple-element.306, s32[10240]{0:T(1024)S(1)} %bitcast.98, s32[512]{0:T(512)S(1)} %bitcast.96, bf16[10240]{0:T(1024)(128)(2,1)S(1)} %reduce.6), kind=kOutput, calls=%fused_computation.20.clone.1 | convolution fusion | flops 681574400 | bytes 1505284 | tf_op jit(solution)/shard_map/while/body/eval_jaxpr/fde,fre->fdr/dot_general | solution.py:92
  146.8 3.4 %fusion.52 = f32[8,1,64,512]{3,2,1,0:T(8,128)S(1)} fusion(f32[8,1,64,512]{3,2,1,0:T(8,128)S(1)} %get-tuple-element.293, s32[]{:T(128)S(6)} %copy.68, bf16[1,64,10240]{2,1,0:T(8,128)(2,1)S(1)} %get-tuple-element.306, s32[10240]{0:T(1024)S(1)} %bitcast.98, s32[512]{0:T(512)S(1)} %bitcast.96, bf16[10240]{0:T(1024)(128)(2,1)S(1)} %reduce.6), kind=kOutput, calls=%fused_computation.20.clone.1 | convolution fusion | flops 681574400 | bytes 1505284 | tf_op jit(solution)/shard_map/while/body/eval_jaxpr/fde,fre->fdr/dot_general | solution.py:92
  151.6 3.4 %fusion.52 = f32[8,1,64,512]{3,2,1,0:T(8,128)S(1)} fusion(f32[8,1,64,512]{3,2,1,0:T(8,128)S(1)} %get-tuple-element.293, s32[]{:T(128)S(6)} %copy.68, bf16[1,64,10240]{2,1,0:T(8,128)(2,1)S(1)} %get-tuple-element.306, s32[10240]{0:T(1024)S(1)} %bitcast.98, s32[512]{0:T(512)S(1)} %bitcast.96, bf16[10240]{0:T(1024)(128)(2,1)S(1)} %reduce.6), kind=kOutput, calls=%fused_computation.20.clone.1 | convolution fusion | flops 681574400 | bytes 1505284 | tf_op jit(solution)/shard_map/while/body/eval_jaxpr/fde,fre->fdr/dot_general | solution.py:92
  156.4 3.4 %fusion.52 = f32[8,1,64,512]{3,2,1,0:T(8,128)S(1)} fusion(f32[8,1,64,512]{3,2,1,0:T(8,128)S(1)} %get-tuple-element.293, s32[]{:T(128)S(6)} %copy.68, bf16[1,64,10240]{2,1,0:T(8,128)(2,1)S(1)} %get-tuple-element.306, s32[10240]{0:T(1024)S(1)} %bitcast.98, s32[512]{0:T(512)S(1)} %bitcast.96, bf16[10240]{0:T(1024)(128)(2,1)S(1)} %reduce.6), kind=kOutput, calls=%fused_computation.20.clone.1 | convolution fusion | flops 681574400 | bytes 1505284 | tf_op jit(solution)/shard_map/while/body/eval_jaxpr/fde,fre->fdr/dot_general | solution.py:92
  161.2 3.4 %fusion.52 = f32[8,1,64,512]{3,2,1,0:T(8,128)S(1)} fusion(f32[8,1,64,512]{3,2,1,0:T(8,128)S(1)} %get-tuple-element.293, s32[]{:T(128)S(6)} %copy.68, bf16[1,64,10240]{2,1,0:T(8,128)(2,1)S(1)} %get-tuple-element.306, s32[10240]{0:T(1024)S(1)} %bitcast.98, s32[512]{0:T(512)S(1)} %bitcast.96, bf16[10240]{0:T(1024)(128)(2,1)S(1)} %reduce.6), kind=kOutput, calls=%fused_computation.20.clone.1 | convolution fusion | flops 681574400 | bytes 1505284 | tf_op jit(solution)/shard_map/while/body/eval_jaxpr/fde,fre->fdr/dot_general | solution.py:92
  166.0 3.4 %fusion.52 = f32[8,1,64,512]{3,2,1,0:T(8,128)S(1)} fusion(f32[8,1,64,512]{3,2,1,0:T(8,128)S(1)} %get-tuple-element.293, s32[]{:T(128)S(6)} %copy.68, bf16[1,64,10240]{2,1,0:T(8,128)(2,1)S(1)} %get-tuple-element.306, s32[10240]{0:T(1024)S(1)} %bitcast.98, s32[512]{0:T(512)S(1)} %bitcast.96, bf16[10240]{0:T(1024)(128)(2,1)S(1)} %reduce.6), kind=kOutput, calls=%fused_computation.20.clone.1 | convolution fusion | flops 681574400 | bytes 1505284 | tf_op jit(solution)/shard_map/while/body/eval_jaxpr/fde,fre->fdr/dot_general | solution.py:92
  169.6 5.4 %all-to-all-done = bf16[1,64,64,160]{3,1,0,2:T(8,128)(2,1)} async-done(((bf16[1,64,64,160]{3,1,0,2:T(8,128)(2,1)}), bf16[1,64,64,160]{3,1,0,2:T(8,128)(2,1)}, u32[]{:S(2)}, u32[]{:S(2)}) %all-to-all-start) | async-done | bytes 1310752 | tf_op jit(solution)/shard_map/all_to_all | solution.py:74
  175.7 4.3 %all-to-all-start.3 = ((f32[4,1,4096]{2,1,0:T(1,128)}), f32[4,1,4096]{2,1,0:T(1,128)S(1)}, u32[]{:S(2)}, u32[]{:S(2)}) async-start(f32[4,1,4096]{2,1,0:T(1,128)} %broadcast_in_dim.58), calls=%async_computation.3 | async-start | bytes 131072 | tf_op jit(solution)/shard_map/all_to_all | solution.py:31
  180.0 7.4 %fusion.37 = f32[1,64,128]{2,1,0:T(8,128)} fusion(s32[64,160]{1,0:T(8,128)S(1)} %bitcast.93, s32[64,160]{1,0:T(8,128)S(1)} %bitcast.89, bf16[1,64,64,160]{3,1,0,2:T(8,128)(2,1)} %all-to-all-done), kind=kOutput, calls=%fused_computation.33 | convolution fusion | flops 171704320 | bytes 1425408 | tf_op jit(solution)/shard_map/fdnk,fnkj->fdj/dot_general | solution.py:81
  (84 shorter events, 16.9 us)
Async XLA Ops:
  0.6 24.7 %copy-start = (bf16[1,64,128]{2,1,0:T(8,128)(2,1)S(1)}, bf16[1,64,128]{2,1,0:T(8,128)(2,1)}, u32[]{:S(2)}) copy-start(bf16[1,64,128]{2,1,0:T(8,128)(2,1)} %param.13) | copy-start | bytes 49156
  3.2 22.1 %all-to-all-start.1 = ((s32[2,1,64,160]{3,0,1,2:T(2,128)}), s32[2,1,64,160]{3,0,1,2:T(2,128)S(1)}, u32[]{:S(2)}, u32[]{:S(2)}) async-start(s32[2,1,64,160]{3,0,1,2:T(2,128)} %copy.43), calls=%async_computation.1 | async-start | bytes 262144 | tf_op jit(solution)/shard_map/all_to_all | solution.py:22
  30.3 82.9 %all-to-all-start.2 = ((bf16[1,64,64,160]{3,1,0,2:T(8,128)(2,1)}), bf16[1,64,64,160]{3,1,0,2:T(8,128)(2,1)S(1)}, u32[]{:S(2)}, u32[]{:S(2)}) async-start(bf16[1,64,64,160]{3,1,0,2:T(8,128)(2,1)} %convert_bitcast_fusion), calls=%async_computation.2 | async-start | bytes 4194304 | tf_op jit(solution)/shard_map/all_to_all | solution.py:86
  36.0 66.4 %copy-start.3 = (s32[1,1,64,160]{3,2,1,0:T(8,128)S(1)}, s32[1,1,64,160]{3,2,1,0:T(8,128)}, u32[]{:S(2)}) copy-start(s32[1,1,64,160]{3,2,1,0:T(8,128)} %param.16) | copy-start | bytes 122884
  102.4 0.7 copy-start.5
  108.6 4.2 %copy-start.8 = (s32[1,1,64]{2,1,0:T(1,128)S(1)}, s32[1,1,64]{2,1,0:T(1,128)}, u32[]{:S(2)}) copy-start(s32[1,1,64]{2,1,0:T(1,128)} %param.17) | copy-start | bytes 772
  108.6 4.5 %copy-start.4 = (s32[1,1,10240]{2,1,0:T(1,128)S(1)}, s32[1,1,10240]{2,1,0:T(1,128)}, u32[]{:S(2)}) copy-start(s32[1,1,10240]{2,1,0:T(1,128)} %reshape.288) | copy-start | bytes 122884
  113.2 61.8 %all-to-all-start = ((bf16[1,64,64,160]{3,1,0,2:T(8,128)(2,1)}), bf16[1,64,64,160]{3,1,0,2:T(8,128)(2,1)}, u32[]{:S(2)}, u32[]{:S(2)}) async-start(bf16[1,64,64,160]{3,1,0,2:T(8,128)(2,1)} %copy.42), calls=%async_computation | async-start | bytes 4194304 | tf_op jit(solution)/shard_map/all_to_all | solution.py:74
  126.3 4.6 %copy-start.1 = (f32[8,1,64,512]{3,2,1,0:T(8,128)S(1)}, f32[8,1,64,512]{3,2,1,0:T(8,128)}, u32[]{:S(2)}) copy-start(f32[8,1,64,512]{3,2,1,0:T(8,128)} %custom-call.1) | copy-start | bytes 3145732
  126.3 4.6 %copy-start.6 = (s32[1,1,10240]{2,1,0:T(1,128)S(1)}, s32[1,1,10240]{2,1,0:T(1,128)}, u32[]{:S(2)}) copy-start(s32[1,1,10240]{2,1,0:T(1,128)} %copy-done.5) | copy-start | bytes 122884
  175.7 11.8 %all-to-all-start.3 = ((f32[4,1,4096]{2,1,0:T(1,128)}), f32[4,1,4096]{2,1,0:T(1,128)S(1)}, u32[]{:S(2)}, u32[]{:S(2)}) async-start(f32[4,1,4096]{2,1,0:T(1,128)} %broadcast_in_dim.58), calls=%async_computation.3 | async-start | bytes 131072 | tf_op jit(solution)/shard_map/all_to_all | solution.py:31
  180.0 7.6 %copy-start.7 = (f32[1,4096]{1,0:T(1,128)S(1)}, f32[1,4096]{1,0:T(1,128)}, u32[]{:S(2)}) copy-start(f32[1,4096]{1,0:T(1,128)} %param.12) | copy-start | bytes 49156
  187.4 1.0 copy-start.2
where the time goes:
time: 191 us; the launch traced here: 189 us
  matrix products  95.9 us (50%)
  starting transfers between devices  32.7 us (17%)
  local copies, waits for them, and re-layouts  28.1 us (15%)
  waiting for transfers between devices  14.4 us (8%)
  loops' own time  10.8 us (6%)
  other arithmetic  6.52 us (3%)
    dot_general x8, matrix products, lookup_block(): jnp.einsum('fdr,fre->fde', table_part, selector, preferred_element_type=j...  56.3 us
    dot_general x8, matrix products, gradient_block(): jnp.einsum('fde,fre->fdr', entry_flat, weighted, preferred_element_type=j...  27.3 us
    all_to_all x1, starting transfers between devices, in_one_piece(): lax.all_to_all(both, axis, split_axis=split_dim, concat_axis=concat_dim,...  12.1 us
    all_to_all x1, starting transfers between devices, shards(): lax.all_to_all(picked, 'rows', split_axis=2, concat_axis=2, tiled=True)  10.6 us
    dynamic_slice x16, local copies, waits for them, and re-layouts, shards(): lax.scan(lookup_block, jnp.zeros((feat_count, dim_local, entry_count), jn...  9.35 us
    all_to_all x1, waiting for transfers between devices, in_one_piece(): lax.all_to_all(both, axis, split_axis=split_dim, concat_axis=concat_dim,...  8.98 us
    reshape x2, local copies, waits for them, and re-layouts, shards(): looked_up.astype(jnp.bfloat16)  7.76 us
    dot_general x1, matrix products, shards(): jnp.einsum('fdnk,fnkj->fdj', arrived_rows, onehot, preferred_element_type...  7.41 us
  transfers between devices with their start and end apart: 4, of which 2 were waited for; matrix products, arithmetic and copies ran while one was open for 64% of the time, Pallas kernels for 0%

commit v1 on v0

v1 whole, which is shorter than its diff:
```python
import jax
import jax.numpy as jnp
from jax import lax
from jax.experimental import pallas as pl
from jax.experimental.pallas import tpu as pltpu
from jax.sharding import PartitionSpec as P

D = 256
STEP = 0.3
H = 8
F32 = jnp.float32
BF = jnp.bfloat16
NT = (((1,), (1,)), ((), ()))
MESH = pl.DeviceIdType.MESH
Z, Y, C, X = 8, 4, 2, 4


def one():
    return jnp.ones((), BF)


def zero():
    return jnp.zeros((), BF)


def lay_out(row_ref, smp_ref, wgt_ref, cnt_ref, rows, slots, weights):
    eye = lax.broadcasted_iota(jnp.int32, (64, 64), 0) == lax.broadcasted_iota(jnp.int32, (64, 64), 1)
    count = jnp.where(eye, jnp.broadcast_to(cnt_ref[...], (64, 64)), 0).astype(F32)
    count = jnp.sum(count, axis=1, keepdims=True).astype(jnp.int32)
    lane = lax.broadcasted_iota(jnp.int32, (64, 128), 1)
    main = jnp.where(lane < count, wgt_ref[:, :128], 0)
    lane = lax.broadcasted_iota(jnp.int32, (64, 32), 1) + 128
    tail = jnp.where(lane < count, wgt_ref[:, 128:160], 0)
    for dst, m, t in (
        (rows, row_ref[:, :128], row_ref[:, 128:160]),
        (slots, smp_ref[:, :128], smp_ref[:, 128:160]),
        (weights, main, tail),
    ):
        dst[0:64, :] = m.astype(F32)
        t = t.astype(F32)
        for k in range(2):
            parts = [t[(4 * k + z) * 8 : (4 * k + z + 1) * 8, :] for z in range(4)]
            dst[64 + 8 * k : 72 + 8 * k, :] = jnp.concatenate(parts, axis=1)


def high_low(r, L):
    h = jnp.floor(r * (1.0 / L))
    return h, r - h * L


def lookup(s, L, rows, slots, weights, t2, oh, xs, put):
    iota = lax.broadcasted_iota(jnp.int32, (256, 128), 0).astype(F32).astype(BF)
    high = []
    for t in range(10):
        h, low = high_low(rows[pl.ds(t * 8 + s, 1), :], L)
        high.append(h)
        for k in range(L // 256):
            key = (low - 256.0 * k).astype(BF)
            oh[k * 256 : (k + 1) * 256, t * 128 : (t + 1) * 128] = jnp.where(iota == key, one(), zero())
    x2 = jnp.dot(t2[...], oh[...], preferred_element_type=F32)
    for t in range(10):
        cols = slice(t * 128, (t + 1) * 128)
        x = x2[0:64, cols]
        for h in range(1, H):
            x = jnp.where(high[t] == float(h), x2[h * 64 : (h + 1) * 64, cols], x)
        x = x.astype(BF)
        if t < 8:
            xs[:, t * 256 : t * 256 + 128] = x
        else:
            for z in range((t - 8) * 4, (t - 8) * 4 + 4):
                xs[:, z * 256 + 128 : z * 256 + 256] = x
    sample = lax.broadcasted_iota(jnp.int32, (128, 128), 0).astype(F32).astype(BF)
    lane = lax.broadcasted_iota(jnp.int32, (1, 128), 1)
    for z in range(8):
        at, tail = z * 8 + s, (8 + z // 4) * 8 + s
        mine = (lane >= 32 * (z % 4)) & (lane < 32 * (z % 4) + 32)
        tail_w = jnp.where(mine, weights[pl.ds(tail, 1), :], 0.0).astype(BF)
        spread = jnp.concatenate(
            [
                jnp.where(sample == slots[pl.ds(at, 1), :].astype(BF), weights[pl.ds(at, 1), :].astype(BF), zero()),
                jnp.where(sample == slots[pl.ds(tail, 1), :].astype(BF), tail_w, zero()),
            ],
            axis=1,
        )
        put(z, lax.dot_general(xs[:, z * 256 : (z + 1) * 256], spread, NT, preferred_element_type=F32))


def gradient(s, L, grad, rows, slots, weights, a, wr, acc):
    iota = lax.broadcasted_iota(jnp.int32, (256, 128), 0).astype(F32).astype(BF)
    lane = lax.broadcasted_iota(jnp.int32, (1, 128), 1)
    for t in range(10):
        cols = slice(t * 128, (t + 1) * 128)
        h, low = high_low(rows[pl.ds(t * 8 + s, 1), :], L)
        h = h.astype(BF)
        w = weights[pl.ds(t * 8 + s, 1), :].astype(BF)
        for k in range(L // 256):
            key = (low - 256.0 * k).astype(BF)
            wr[k * 256 : (k + 1) * 256, cols] = jnp.where(iota == key, w, zero())
        index = jnp.broadcast_to(slots[pl.ds(t * 8 + s, 1), :].astype(jnp.int32), (64, 128))

        def pick(z):
            return jnp.take_along_axis(grad(z).astype(F32), index, axis=1, mode="promise_in_bounds")

        if t < 8:
            e = pick(t)
        else:
            e = pick((t - 8) * 4)
            for z in range(1, 4):
                e = jnp.where(lane >= 32 * z, pick((t - 8) * 4 + z), e)
        e = e.astype(BF)
        for k in range(H):
            a[k * 64 : (k + 1) * 64, cols] = jnp.where(h == jnp.asarray(float(k), BF), e, zero())
    acc[...] += lax.dot_general(a[...], wr[...], NT, preferred_element_type=F32)


def kernel(
    tab, accum, g, smp, row, wgt, cnt,
    pooled, new_tab, new_accum,
    rows, slots, weights, t2, oh, xs, a, acc,
    gall, part, from_core, from_y, from_z, squares,
    gz_s, gz_r, gy_s, gy_r, gc_s, gc_r, pc_s, pc_r, py_s, py_r, pz_s, pz_r, sx_s, sx_r,
):
    L = tab.shape[1] // H
    r, x = lax.axis_index("rows"), lax.axis_index("dims")
    z, y, c = r // (Y * C), lax.rem(r // C, Y), lax.rem(r, C)

    def z_at(d):
        return (lax.rem(z + d, Z) * (Y * C) + y * C + c, x)

    def y_at(d):
        return (z * (Y * C) + lax.rem(y + d, Y) * C + c, x)

    def x_at(d):
        return (r, lax.rem(x + d, X))

    sibling = (z * (Y * C) + y * C + (1 - c), x)

    def copy(src, dst, send, recv, to):
        return pltpu.make_async_remote_copy(
            src_ref=src, dst_ref=dst, send_sem=send, recv_sem=recv, device_id=to, device_id_type=MESH
        )

    barrier = pltpu.get_barrier_semaphore()
    peers = [z_at(d) for d in range(1, Z)] + [y_at(d) for d in range(1, Y)] + [sibling]
    peers += [x_at(d) for d in range(1, X)]
    for to in peers:
        pl.semaphore_signal(barrier, inc=1, device_id=to, device_id_type=MESH)

    gall[c, y, z] = g[...]
    lay_out(row, smp, wgt, cnt, rows, slots, weights)
    for h in range(H):
        t2[h * 64 : (h + 1) * 64, :] = tab[:, h * L : (h + 1) * L]
    acc[...] = jnp.zeros_like(acc)

    pl.semaphore_wait(barrier, len(peers))

    along_z = [
        copy(g, gall.at[c, y, z], gz_s.at[d - 1], gz_r.at[d - 1], z_at(d)) for d in range(1, Z)
    ]
    along_y = [
        copy(gall.at[c, y], gall.at[c, y], gy_s.at[d - 1], gy_r.at[d - 1], y_at(d)) for d in range(1, Y)
    ]
    to_core = copy(gall.at[c], gall.at[c], gc_s.at[0], gc_r.at[0], sibling)
    for each in along_z:
        each.start()

    def look(q, side):
        block = lax.rem(y + 1 + q, Y)

        def put(k, value):
            part[side, block, k] = value

        lookup(block * C + side, L, rows, slots, weights, t2, oh, xs, put)
        return block

    def to_sibling(q):
        block = lax.rem(y + 1 + q, Y)
        return copy(part.at[1 - c, block], from_core.at[q], pc_s.at[q], pc_r.at[q], sibling)

    def to_y(q):
        return copy(
            part.at[c, lax.rem(y + 1 + q, Y)], from_y.at[q], py_s.at[q], py_r.at[q], y_at(q + 1)
        )

    def to_z(d):
        return copy(
            part.at[c, y, lax.rem(z + d, Z)], from_z.at[d - 1], pz_s.at[d - 1], pz_r.at[d - 1], z_at(d)
        )

    @pl.loop(0, 2 * Y)
    def _(i):
        q = lax.rem(i, Y)
        side = jnp.where(i < Y, 1 - c, c)
        block = look(q, side)

        @pl.when(i < Y)
        def _():
            to_sibling(q).start()

        @pl.when(i >= Y)
        def _():
            to_sibling(q).wait_recv()
            part[c, block] += from_core[q]

        @pl.when((i >= Y) & (i < 2 * Y - 1))
        def _():
            to_y(q).start()

        @pl.when(i == 2)
        def _():
            for each in along_z:
                each.wait_recv()
            for each in along_y:
                each.start()

        @pl.when(i == 5)
        def _():
            for each in along_y:
                each.wait_recv()
            to_core.start()

    @pl.loop(0, 2 * Y)
    def _(i):
        side = jnp.where(i < Y, c, 1 - c)
        block = lax.rem(i, Y)

        @pl.when(i == Y)
        def _():
            to_core.wait_recv()

        @pl.when(i == 3)
        def _():
            for q in range(Y - 1):
                to_y(q).wait_recv()
            part[c, y] += from_y[0] + from_y[1] + from_y[2]
            for d in range(1, Z):
                to_z(d).start()

        gradient(block * C + side, L, lambda k: gall[side, block, k], rows, slots, weights, a, oh, acc)

    for h in range(H):
        v = acc[h * 64 : (h + 1) * 64, :]
        squares[x, h : h + 1, :] = jnp.sum(v * v, axis=0, keepdims=True)
    along_x = [
        copy(squares.at[x], squares.at[x], sx_s.at[d - 1], sx_r.at[d - 1], x_at(d)) for d in range(1, X)
    ]
    for each in along_x:
        each.start()

    for d in range(1, Z):
        to_z(d).wait_recv()
    total = part[c, y, z]
    for d in range(1, Z):
        total += from_z[d - 1]
    pooled[...] = total

    for each in along_x:
        each.wait_recv()
    norm = (squares[0] + squares[1]) + (squares[2] + squares[3])
    for h in range(H):
        cols = slice(h * L, (h + 1) * L)
        new = accum[:, cols] + norm[h : h + 1, :] / D
        new_accum[:, cols] = new
        moved = acc[h * 64 : (h + 1) * 64, :] * (STEP * lax.rsqrt(new))
        new_tab[:, cols] = (tab[:, cols].astype(F32) - moved).astype(BF)

    for each in along_z + along_y + [to_core] + along_x:
        each.wait_send()
    for q in range(Y):
        to_sibling(q).wait_send()
    for q in range(Y - 1):
        to_y(q).wait_send()
    for d in range(1, Z):
        to_z(d).wait_send()


def shards(table, accum, grad_pooled, sample_slot, row_slot, weight, send_count):
    _, dim, n_rows = table.shape
    own = grad_pooled.shape[2]
    L = n_rows // H
    vmem = pl.BlockSpec(memory_space=pltpu.VMEM)
    dma = pltpu.SemaphoreType.DMA
    pooled, new_table, new_accum = pl.pallas_call(
        kernel,
        out_shape=(
            jax.ShapeDtypeStruct((dim, own), F32),
            jax.ShapeDtypeStruct((dim, n_rows), BF),
            jax.ShapeDtypeStruct((1, n_rows), F32),
        ),
        in_specs=[vmem] * 7,
        out_specs=(vmem,) * 3,
        scratch_shapes=[pltpu.VMEM((80, 128), F32)] * 3
        + [
            pltpu.VMEM((64 * H, L), BF),
            pltpu.VMEM((L, 1280), BF),
            pltpu.VMEM((64, 2048), BF),
            pltpu.VMEM((64 * H, 1280), BF),
            pltpu.VMEM((64 * H, L), F32),
            pltpu.VMEM((C, Y, Z, dim, own), BF),
            pltpu.VMEM((C, Y, Z, dim, own), F32),
            pltpu.VMEM((Y, Z, dim, own), F32),
            pltpu.VMEM((Y - 1, Z, dim, own), F32),
            pltpu.VMEM((Z - 1, dim, own), F32),
            pltpu.VMEM((X, H, L), F32),
        ]
        + [dma((n,)) for n in (7, 7, 3, 3, 1, 1, 4, 4, 3, 3, 7, 7, 3, 3)],
        compiler_params=pltpu.CompilerParams(
            collective_id=0, has_side_effects=True, vmem_limit_bytes=40 << 20
        ),
    )(
        table[0],
        accum,
        grad_pooled[0],
        sample_slot[0, 0],
        row_slot[0, 0],
        weight[0, 0],
        send_count[0],
    )
    return pooled[None], new_table[None], new_accum


def solution(mesh):
    return jax.shard_map(
        shards,
        mesh=mesh,
        in_specs=(
            P(None, "dims", "rows"),
            P(None, "rows"),
            P(None, "dims", "rows"),
            P(None, "rows", None, None),
            P(None, "rows", None, None),
            P(None, "rows", None, None),
            P(None, "rows", None),
        ),
        out_specs=(P(None, "dims", "rows"), P(None, "dims", "rows"), P(None, "rows")),
        check_vma=False,
    )
```

time: 191 us -> 51.3 us (0.27)
  matrix products: 95.9 us -> 0 us
  Pallas kernels: 0 us -> 42.1 us
  starting transfers between devices: 32.7 us -> 0 us
  local copies, waits for them, and re-layouts: 28.1 us -> 7.65 us
  waiting for transfers between devices: 14.4 us -> 0 us
  loops' own time: 10.8 us -> 0 us
  other arithmetic: 6.52 us -> 0 us
    dot_general x18 -> x0, matrix products: 95.9 us -> none  [the longest x8 56.3 us: lookup_block(): jnp.einsum('fdr,fre->fde', table_part, selector, preferred_element_type=j...]
    pallas_call x0 -> x1, Pallas kernels: none -> 42.1 us  [shards(): pl.pallas_call(kernel, out_shape=(jax.ShapeDtypeStruct((dim, own), F32),...]
    all_to_all x4 -> x0, starting transfers between devices: 32.7 us -> none  [the longest x1 12.1 us: in_one_piece(): lax.all_to_all(both, axis, split_axis=split_dim, concat_axis=concat_dim,...]
    all_to_all x4 -> x0, waiting for transfers between devices: 14.4 us -> none  [the longest x1 8.98 us: in_one_piece(): lax.all_to_all(both, axis, split_axis=split_dim, concat_axis=concat_dim,...]
    reshape x4 -> x0, local copies, waits for them, and re-layouts: 13.1 us -> none  [the longest x2 7.76 us: shards(): looked_up.astype(jnp.bfloat16)]
    another operation x2 -> x0, loops' own time: 10.8 us -> none  [the longest x1 5.46 us: shards(): lax.map(gradient_block, jnp.arange(block_count, dtype=jnp.int32))]
    dynamic_slice x16 -> x0, local copies, waits for them, and re-layouts: 9.35 us -> none  [shards(): lax.scan(lookup_block, jnp.zeros((feat_count, dim_local, entry_count), jn...]
    unnamed x21 -> x17, local copies, waits for them, and re-layouts: 0.26 us -> 7.65 us
  transfers between devices with their start and end apart: 4 -> 0, of which waited for: 2 -> 0; matrix products, arithmetic and copies ran while one was open for 64% -> 0% of each run, Pallas kernels for 0% -> 0%
where the time goes in v1:
time: 51.3 us; the launch traced here: 50.4 us
  Pallas kernels  42.1 us (82%)
  local copies, waits for them, and re-layouts  7.65 us (15%)
  between operations  0.66 us (1%)
    pallas_call x1, Pallas kernels, shards(): pl.pallas_call(kernel, out_shape=(jax.ShapeDtypeStruct((dim, own), F32),...  42.1 us
    unnamed x17, local copies, waits for them, and re-layouts  7.65 us

profile of v1, /device:TPU:8, one launch (start us, length us, event | category | flops | bytes accessed | tf_op | source)
XLA Modules:
  0.0 50.4 jit_solution(137576246274747946)
XLA Ops:
  0.6 0.0 copy-start.6
  0.6 0.6 %copy-done.6 = s32[1,1,64]{2,1,0:T(1,128)S(1)} copy-done((s32[1,1,64]{2,1,0:T(1,128)S(1)}, s32[1,1,64]{2,1,0:T(1,128)}, u32[]{:S(2)}) %copy-start.6) | copy-done | bytes 280
  1.3 0.0 copy-start
  1.3 1.0 %copy-done = bf16[1,64,4096]{2,1,0:T(8,128)(2,1)S(1)} copy-done((bf16[1,64,4096]{2,1,0:T(8,128)(2,1)S(1)}, bf16[1,64,4096]{2,1,0:T(8,128)(2,1)}, u32[]{:S(2)}) %copy-start) | copy-done | bytes 524312
  2.3 0.0 copy-start.1
  2.3 0.8 %copy-done.1 = s32[1,1,64,160]{3,2,1,0:T(8,128)S(1)} copy-done((s32[1,1,64,160]{3,2,1,0:T(8,128)S(1)}, s32[1,1,64,160]{3,2,1,0:T(8,128)}, u32[]{:S(2)}) %copy-start.1) | copy-done | bytes 40984
  3.2 0.0 copy-start.2
  3.2 0.8 %copy-done.2 = s32[1,1,64,160]{3,2,1,0:T(8,128)S(1)} copy-done((s32[1,1,64,160]{3,2,1,0:T(8,128)S(1)}, s32[1,1,64,160]{3,2,1,0:T(8,128)}, u32[]{:S(2)}) %copy-start.2) | copy-done | bytes 40984
  4.0 0.0 copy-start.3
  4.0 0.8 %copy-done.3 = s32[1,1,64,160]{3,2,1,0:T(8,128)S(1)} copy-done((s32[1,1,64,160]{3,2,1,0:T(8,128)S(1)}, s32[1,1,64,160]{3,2,1,0:T(8,128)}, u32[]{:S(2)}) %copy-start.3) | copy-done | bytes 40984
  4.9 0.0 copy-start.4
  4.9 0.7 %copy-done.4 = f32[1,4096]{1,0:T(1,128)S(1)} copy-done((f32[1,4096]{1,0:T(1,128)S(1)}, f32[1,4096]{1,0:T(1,128)}, u32[]{:S(2)}) %copy-start.4) | copy-done | bytes 16408
  5.6 0.0 copy-start.5
  5.6 0.7 %copy-done.5 = bf16[1,64,128]{2,1,0:T(8,128)(2,1)S(1)} copy-done((bf16[1,64,128]{2,1,0:T(8,128)(2,1)S(1)}, bf16[1,64,128]{2,1,0:T(8,128)(2,1)}, u32[]{:S(2)}) %copy-start.5) | copy-done | bytes 16408
  6.3 42.1 %shard_map.94 = (f32[64,128]{1,0:T(8,128)S(1)}, bf16[64,4096]{1,0:T(8,128)(2,1)S(1)}, f32[1,4096]{1,0:T(1,128)S(1)}) custom-call(bf16[64,4096]{1,0:T(8,128)(2,1)S(1)} %bitcast.8, f32[1,4096]{1,0:T(1,128)S(1)} %copy-done.4, bf16[64,128]{1,0:T(8,128)(2,1)S(1)} %bitcast.14, s32[64,160]{1,0:T(8,128)S(1)} %bitcast.10, s32[64,160]{1,0:T(8,128)S(1)} %bitcast.11, ...), custom_call_target="tpu_custom_call" | custom-call | tf_op jit(solution)/shard_map/pallas_call | solution.py:283
  48.4 0.6 %copy.13 = f32[1,64,128]{2,1,0:T(8,128)} copy(f32[1,64,128]{2,1,0:T(8,128)S(1)} %bitcast.13) | data formatting | bytes 65536
  49.0 0.8 %copy.14 = bf16[1,64,4096]{2,1,0:T(8,128)(2,1)} copy(bf16[1,64,4096]{2,1,0:T(8,128)(2,1)S(1)} %bitcast.9) | data formatting | bytes 1048576
  49.8 0.6 %copy.15 = f32[1,4096]{1,0:T(1,128)} copy(f32[1,4096]{1,0:T(1,128)S(1)} %get-tuple-element.14) | data formatting | bytes 32768
Async XLA Ops:
  0.6 0.7 %copy-start.6 = (s32[1,1,64]{2,1,0:T(1,128)S(1)}, s32[1,1,64]{2,1,0:T(1,128)}, u32[]{:S(2)}) copy-start(s32[1,1,64]{2,1,0:T(1,128)} %param.13) | copy-start | bytes 772
  1.3 1.0 %copy-start = (bf16[1,64,4096]{2,1,0:T(8,128)(2,1)S(1)}, bf16[1,64,4096]{2,1,0:T(8,128)(2,1)}, u32[]{:S(2)}) copy-start(bf16[1,64,4096]{2,1,0:T(8,128)(2,1)} %param.7) | copy-start | bytes 1572868
  2.3 0.8 %copy-start.1 = (s32[1,1,64,160]{3,2,1,0:T(8,128)S(1)}, s32[1,1,64,160]{3,2,1,0:T(8,128)}, u32[]{:S(2)}) copy-start(s32[1,1,64,160]{3,2,1,0:T(8,128)} %param.10) | copy-start | bytes 122884
  3.2 0.8 %copy-start.2 = (s32[1,1,64,160]{3,2,1,0:T(8,128)S(1)}, s32[1,1,64,160]{3,2,1,0:T(8,128)}, u32[]{:S(2)}) copy-start(s32[1,1,64,160]{3,2,1,0:T(8,128)} %param.11) | copy-start | bytes 122884
  4.0 0.8 %copy-start.3 = (s32[1,1,64,160]{3,2,1,0:T(8,128)S(1)}, s32[1,1,64,160]{3,2,1,0:T(8,128)}, u32[]{:S(2)}) copy-start(s32[1,1,64,160]{3,2,1,0:T(8,128)} %param.12) | copy-start | bytes 122884
  4.9 0.7 %copy-start.4 = (f32[1,4096]{1,0:T(1,128)S(1)}, f32[1,4096]{1,0:T(1,128)}, u32[]{:S(2)}) copy-start(f32[1,4096]{1,0:T(1,128)} %accum.1) | copy-start | bytes 49156
  5.6 0.7 %copy-start.5 = (bf16[1,64,128]{2,1,0:T(8,128)(2,1)S(1)}, bf16[1,64,128]{2,1,0:T(8,128)(2,1)}, u32[]{:S(2)}) copy-start(bf16[1,64,128]{2,1,0:T(8,128)(2,1)} %param.9) | copy-start | bytes 49156

commit v2 on v1

--- a/solution.py
+++ b/solution.py
@@ -114,13 +114,17 @@
 
 
 def kernel(
-    tab, accum, g, smp, row, wgt, cnt,
-    pooled, new_tab, new_accum,
-    rows, slots, weights, t2, oh, xs, a, acc,
+    tab_in, accum_in, g, smp_in, row_in, wgt_in, cnt_in,
+    pooled_out, new_tab_out, new_accum_out,
+    pooled, new_tab, new_accum, store, rows, slots, weights, t2, oh, xs, a, acc,
     gall, part, from_core, from_y, from_z, squares,
-    gz_s, gz_r, gy_s, gy_r, gc_s, gc_r, pc_s, pc_r, py_s, py_r, pz_s, pz_r, sx_s, sx_r,
+    tab, accum, smp, row, wgt, cnt, load, gz_s, gz_r, gy_s, gy_r, gc_s, gc_r, pc_s, pc_r, py_s, py_r, pz_s, pz_r, sx_s, sx_r,
 ):
     L = tab.shape[1] // H
+    pairs = ((cnt_in, cnt), (wgt_in, wgt), (row_in, row), (smp_in, smp), (tab_in, tab), (accum_in, accum))
+    loads = [pltpu.make_async_copy(src, dst, load.at[i]) for i, (src, dst) in enumerate(pairs)]
+    for each in loads:
+        each.start()
     r, x = lax.axis_index("rows"), lax.axis_index("dims")
     z, y, c = r // (Y * C), lax.rem(r // C, Y), lax.rem(r, C)
 
@@ -146,41 +150,54 @@
     for to in peers:
         pl.semaphore_signal(barrier, inc=1, device_id=to, device_id_type=MESH)
 
-    gall[c, y, z] = g[...]
+    own_grad = pltpu.make_async_copy(g, gall.at[c, y, z], load.at[len(pairs)])
+    own_grad.start()
+    acc[...] = jnp.zeros_like(acc)
+    for each in loads:
+        each.wait()
+    own_grad.wait()
     lay_out(row, smp, wgt, cnt, rows, slots, weights)
     for h in range(H):
         t2[h * 64 : (h + 1) * 64, :] = tab[:, h * L : (h + 1) * L]
-    acc[...] = jnp.zeros_like(acc)
 
     pl.semaphore_wait(barrier, len(peers))
 
     along_z = [
-        copy(g, gall.at[c, y, z], gz_s.at[d - 1], gz_r.at[d - 1], z_at(d)) for d in range(1, Z)
-    ]
+        copy(gall.at[c, y, z], gall.at[c, y, z], gz_s.at[d - 1], gz_r.at[d - 1], z_at(d)) for d in range(1, Z)
+    ]
+
+    def block_at(d):
+        return lax.rem(y + d, Y)
+
+    half = (pl.ds(0, Z // 2), pl.ds(Z // 2, Z // 2))
     along_y = [
-        copy(gall.at[c, y], gall.at[c, y], gy_s.at[d - 1], gy_r.at[d - 1], y_at(d)) for d in range(1, Y)
-    ]
-    to_core = copy(gall.at[c], gall.at[c], gc_s.at[0], gc_r.at[0], sibling)
+        copy(gall.at[c, y], gall.at[c, y], gy_s.at[0], gy_r.at[0], y_at(1)),
+        copy(gall.at[c, y], gall.at[c, y], gy_s.at[1], gy_r.at[1], y_at(3)),
+    ]
+    further = [
+        copy(gall.at[c, block_at(3), half[0]], gall.at[c, block_at(3), half[0]], gy_s.at[2], gy_r.at[2], y_at(1)),
+        copy(gall.at[c, block_at(1), half[1]], gall.at[c, block_at(1), half[1]], gy_s.at[3], gy_r.at[3], y_at(3)),
+    ]
+
+    def to_core(k):
+        block = block_at((0, 1, 3, 2)[k])
+        return copy(gall.at[c, block], gall.at[c, block], gc_s.at[k], gc_r.at[k], sibling)
+
     for each in along_z:
         each.start()
 
-    def look(q, side):
-        block = lax.rem(y + 1 + q, Y)
-
-        def put(k, value):
-            part[side, block, k] = value
-
-        lookup(block * C + side, L, rows, slots, weights, t2, oh, xs, put)
-        return block
-
     def to_sibling(q):
-        block = lax.rem(y + 1 + q, Y)
+        block = block_at(jnp.where(q < 2, q + 2, 3 - q))
         return copy(part.at[1 - c, block], from_core.at[q], pc_s.at[q], pc_r.at[q], sibling)
 
-    def to_y(q):
-        return copy(
-            part.at[c, lax.rem(y + 1 + q, Y)], from_y.at[q], py_s.at[q], py_r.at[q], y_at(q + 1)
-        )
+    two_on = [
+        copy(part.at[c, block_at(2), half[0]], from_y.at[0, half[0]], py_s.at[0], py_r.at[0], y_at(1)),
+        copy(part.at[c, block_at(2), half[1]], from_y.at[0, half[1]], py_s.at[1], py_r.at[1], y_at(3)),
+    ]
+    one_on = [
+        copy(part.at[c, block_at(1)], from_y.at[1], py_s.at[2], py_r.at[2], y_at(1)),
+        copy(part.at[c, block_at(3)], from_y.at[2], py_s.at[3], py_r.at[3], y_at(3)),
+    ]
 
     def to_z(d):
         return copy(
@@ -191,7 +208,12 @@
     def _(i):
         q = lax.rem(i, Y)
         side = jnp.where(i < Y, 1 - c, c)
-        block = look(q, side)
+        block = block_at(jnp.where(q < 2, q + 2, 3 - q))
+
+        def put(k, value):
+            part[side, block, k] = value
+
+        lookup(block * C + side, L, rows, slots, weights, t2, oh, xs, put)
 
         @pl.when(i < Y)
         def _():
@@ -202,41 +224,64 @@
             to_sibling(q).wait_recv()
             part[c, block] += from_core[q]
 
-        @pl.when((i >= Y) & (i < 2 * Y - 1))
-        def _():
-            to_y(q).start()
-
-        @pl.when(i == 2)
+        @pl.when(i == 3)
         def _():
             for each in along_z:
                 each.wait_recv()
             for each in along_y:
                 each.start()
-
-        @pl.when(i == 5)
+            to_core(0).start()
+
+        @pl.when(i == Y)
+        def _():
+            for each in two_on:
+                each.start()
+
+        @pl.when(i == 6)
         def _():
             for each in along_y:
                 each.wait_recv()
-            to_core.start()
+            for each in further:
+                each.start()
+            to_core(1).start()
+            to_core(2).start()
+            two_on[1].wait_recv()
+            part[c, block_at(3), half[1]] += from_y[0, half[1]]
+            one_on[1].start()
+
+        @pl.when(i == 7)
+        def _():
+            two_on[0].wait_recv()
+            part[c, block_at(1), half[0]] += from_y[0, half[0]]
+            one_on[0].start()
 
     @pl.loop(0, 2 * Y)
     def _(i):
+        k = lax.rem(i, Y)
         side = jnp.where(i < Y, c, 1 - c)
-        block = lax.rem(i, Y)
-
-        @pl.when(i == Y)
-        def _():
-            to_core.wait_recv()
+        block = block_at(jnp.where(k < 2, k, 5 - k))
 
         @pl.when(i == 3)
         def _():
-            for q in range(Y - 1):
-                to_y(q).wait_recv()
-            part[c, y] += from_y[0] + from_y[1] + from_y[2]
+            for each in further:
+                each.wait_recv()
+            to_core(3).start()
+
+        for n in range(Y):
+
+            @pl.when(i == Y + n)
+            def _():
+                to_core(n).wait_recv()
+
+        gradient(block * C + side, L, lambda n: gall[side, block, n], rows, slots, weights, a, oh, acc)
+
+        @pl.when(i == 5)
+        def _():
+            for each in one_on:
+                each.wait_recv()
+            part[c, y] += from_y[1] + from_y[2]
             for d in range(1, Z):
                 to_z(d).start()
-
-        gradient(block * C + side, L, lambda k: gall[side, block, k], rows, slots, weights, a, oh, acc)
 
     for h in range(H):
         v = acc[h * 64 : (h + 1) * 64, :]
@@ -253,6 +298,8 @@
     for d in range(1, Z):
         total += from_z[d - 1]
     pooled[...] = total
+    out = [pltpu.make_async_copy(pooled, pooled_out, store.at[0])]
+    out[0].start()
 
     for each in along_x:
         each.wait_recv()
@@ -263,33 +310,57 @@
         new_accum[:, cols] = new
         moved = acc[h * 64 : (h + 1) * 64, :] * (STEP * lax.rsqrt(new))
         new_tab[:, cols] = (tab[:, cols].astype(F32) - moved).astype(BF)
-
-    for each in along_z + along_y + [to_core] + along_x:
+    out += [
+        pltpu.make_async_copy(new_tab, new_tab_out, store.at[1]),
+        pltpu.make_async_copy(new_accum, new_accum_out, store.at[2]),
+    ]
+    out[1].start()
+    out[2].start()
+
+    for each in along_z + along_y + further + two_on + one_on + along_x:
         each.wait_send()
     for q in range(Y):
+        to_core(q).wait_send()
         to_sibling(q).wait_send()
-    for q in range(Y - 1):
-        to_y(q).wait_send()
     for d in range(1, Z):
         to_z(d).wait_send()
+    for each in out:
+        each.wait()
+
+
+def hand_on(*refs):
+    n = (len(refs) - 2) // 3
+    src, dst, held, come, go = refs[:n], refs[n : 2 * n], refs[2 * n : 3 * n], refs[-2], refs[-1]
+    loads = [pltpu.make_async_copy(src[i], held[i], come.at[i]) for i in range(n)]
+    stores = [pltpu.make_async_copy(held[i], dst[i], go.at[i]) for i in range(n)]
+    for each in loads:
+        each.start()
+    for i in range(n):
+        loads[i].wait()
+        stores[i].start()
+    for each in stores:
+        each.wait()
 
 
 def shards(table, accum, grad_pooled, sample_slot, row_slot, weight, send_count):
     _, dim, n_rows = table.shape
     own = grad_pooled.shape[2]
     L = n_rows // H
-    vmem = pl.BlockSpec(memory_space=pltpu.VMEM)
     dma = pltpu.SemaphoreType.DMA
-    pooled, new_table, new_accum = pl.pallas_call(
+    anywhere = pl.BlockSpec(memory_space=pl.ANY)
+    shapes = (
+        jax.ShapeDtypeStruct((dim, own), F32),
+        jax.ShapeDtypeStruct((dim, n_rows), BF),
+        jax.ShapeDtypeStruct((1, n_rows), F32),
+    )
+    results = pl.pallas_call(
         kernel,
-        out_shape=(
-            jax.ShapeDtypeStruct((dim, own), F32),
-            jax.ShapeDtypeStruct((dim, n_rows), BF),
-            jax.ShapeDtypeStruct((1, n_rows), F32),
-        ),
-        in_specs=[vmem] * 7,
-        out_specs=(vmem,) * 3,
-        scratch_shapes=[pltpu.VMEM((80, 128), F32)] * 3
+        out_shape=shapes,
+        in_specs=[anywhere] * 7,
+        out_specs=(anywhere,) * 3,
+        scratch_shapes=[pltpu.VMEM(each.shape, each.dtype) for each in shapes]
+        + [dma((3,))]
+        + [pltpu.VMEM((80, 128), F32)] * 3
         + [
             pltpu.VMEM((64 * H, L), BF),
             pltpu.VMEM((L, 1280), BF),
@@ -299,13 +370,16 @@
             pltpu.VMEM((C, Y, Z, dim, own), BF),
             pltpu.VMEM((C, Y, Z, dim, own), F32),
             pltpu.VMEM((Y, Z, dim, own), F32),
-            pltpu.VMEM((Y - 1, Z, dim, own), F32),
+            pltpu.VMEM((3, Z, dim, own), F32),
             pltpu.VMEM((Z - 1, dim, own), F32),
             pltpu.VMEM((X, H, L), F32),
         ]
-        + [dma((n,)) for n in (7, 7, 3, 3, 1, 1, 4, 4, 3, 3, 7, 7, 3, 3)],
+        + [pltpu.VMEM((dim, n_rows), BF), pltpu.VMEM((1, n_rows), F32)]
+        + [pltpu.VMEM(sample_slot.shape[2:], jnp.int32)] * 3
+        + [pltpu.VMEM(send_count.shape[1:], jnp.int32)]
+        + [dma((n,)) for n in (7, 7, 7, 4, 4, 4, 4, 4, 4, 4, 4, 7, 7, 3, 3)],
         compiler_params=pltpu.CompilerParams(
-            collective_id=0, has_side_effects=True, vmem_limit_bytes=40 << 20
+            collective_id=0, has_side_effects=True, vmem_limit_bytes=64 << 20
         ),
     )(
         table[0],
@@ -316,6 +390,14 @@
         weight[0, 0],
         send_count[0],
     )
+    pooled, new_table, new_accum = pl.pallas_call(
+        hand_on,
+        out_shape=shapes,
+        in_specs=[anywhere] * 3,
+        out_specs=(anywhere,) * 3,
+        scratch_shapes=[pltpu.VMEM(each.shape, each.dtype) for each in shapes] + [dma((3,)), dma((3,))],
+        compiler_params=pltpu.CompilerParams(vmem_limit_bytes=64 << 20),
+    )(*results)
     return pooled[None], new_table[None], new_accum
 
 

time: 51.3 us -> 41.2 us (0.80)
  local copies, waits for them, and re-layouts: 7.65 us -> 0 us
  Pallas kernels: 42.1 us -> 40 us
    unnamed x17 -> x0, local copies, waits for them, and re-layouts: 7.65 us -> none
    pallas_call x1 -> x2, Pallas kernels: 42.1 us -> 40 us  [the longest x1 38.1 us: shards(): pl.pallas_call(kernel, out_shape=shapes, in_specs=[anywhere] * 7, out_spe...]
where the time goes in v2:
time: 41.2 us; the launch traced here: 40.7 us
  Pallas kernels  40 us (97%)
  between operations  0.64 us (2%)
    pallas_call x1, Pallas kernels, shards(): pl.pallas_call(kernel, out_shape=shapes, in_specs=[anywhere] * 7, out_spe...  38.1 us
    pallas_call x1, Pallas kernels, shards(): pl.pallas_call(hand_on, out_shape=shapes, in_specs=[anywhere] * 3, out_sp...  1.91 us

profile of v2, /device:TPU:8, one launch (start us, length us, event | category | flops | bytes accessed | tf_op | source)
XLA Modules:
  0.0 40.7 jit_solution(10503092239963735747)
XLA Ops:
  0.6 38.1 %shard_map.94 = (f32[64,128]{1,0:T(8,128)}, bf16[64,4096]{1,0:T(8,128)(2,1)}, f32[1,4096]{1,0:T(1,128)}) custom-call(bf16[64,4096]{1,0:T(8,128)(2,1)} %bitcast.8, f32[1,4096]{1,0:T(1,128)} %accum_in.1, bf16[64,128]{1,0:T(8,128)(2,1)} %bitcast.12, s32[64,160]{1,0:T(8,128)} %bitcast.9, s32[64,160]{1,0:T(8,128)} %bitcast.10, s32[64,160]{1,0:T(8,128)} %bitcast.11, ...), custom_call_target="tpu_custom_call" | custom-call | tf_op jit(solution)/shard_map/pallas_call | solution.py:356
  38.8 1.9 %shard_map.95 = (f32[64,128]{1,0:T(8,128)}, bf16[64,4096]{1,0:T(8,128)(2,1)}, f32[1,4096]{1,0:T(1,128)}) custom-call(f32[64,128]{1,0:T(8,128)} %get-tuple-element.9.refs_0_, bf16[64,4096]{1,0:T(8,128)(2,1)} %get-tuple-element.10.refs_1_, f32[1,4096]{1,0:T(1,128)} %get-tuple-element.11.refs_2_), custom_call_target="tpu_custom_call" | custom-call | tf_op jit(solution)/shard_map/pallas_call | solution.py:393

commit v3 on v2

--- a/solution.py
+++ b/solution.py
@@ -113,11 +113,32 @@
     acc[...] += lax.dot_general(a[...], wr[...], NT, preferred_element_type=F32)
 
 
+def pack(values, dst):
+    n, dim, own = values.shape
+    row = lax.broadcasted_iota(jnp.int32, (16, own), 0)
+    exponents = jnp.zeros((16, own), F32)
+    for j in range(n):
+        top = jnp.max(jnp.abs(values[j]), axis=0, keepdims=True)
+        e = jnp.ceil(jnp.log2(jnp.maximum(top, 1e-30)))
+        dst[j * dim : (j + 1) * dim, :] = jnp.round(values[j] * jnp.exp2(14.0 - e)).astype(jnp.int32).astype(jnp.int16)
+        exponents = jnp.where(row == j, e, exponents)
+    dst[n * dim : n * dim + 16, :] = exponents.astype(jnp.int32).astype(jnp.int16)
+
+
+def unpack(src, n):
+    dim = (src.shape[0] - 16) // n
+    exponents = src[n * dim : n * dim + 16, :].astype(jnp.int32).astype(F32)
+    return [
+        src[j * dim : (j + 1) * dim, :].astype(jnp.int32).astype(F32) * jnp.exp2(exponents[j : j + 1, :] - 14.0)
+        for j in range(n)
+    ]
+
+
 def kernel(
     tab_in, accum_in, g, smp_in, row_in, wgt_in, cnt_in,
     pooled_out, new_tab_out, new_accum_out,
     pooled, new_tab, new_accum, store, rows, slots, weights, t2, oh, xs, a, acc,
-    gall, part, from_core, from_y, from_z, squares,
+    gall, part, from_core, two_out, two_in, one_out, one_in, z_out, z_in, squares,
     tab, accum, smp, row, wgt, cnt, load, gz_s, gz_r, gy_s, gy_r, gc_s, gc_r, pc_s, pc_r, py_s, py_r, pz_s, pz_r, sx_s, sx_r,
 ):
     L = tab.shape[1] // H
@@ -153,13 +174,7 @@
     own_grad = pltpu.make_async_copy(g, gall.at[c, y, z], load.at[len(pairs)])
     own_grad.start()
     acc[...] = jnp.zeros_like(acc)
-    for each in loads:
-        each.wait()
     own_grad.wait()
-    lay_out(row, smp, wgt, cnt, rows, slots, weights)
-    for h in range(H):
-        t2[h * 64 : (h + 1) * 64, :] = tab[:, h * L : (h + 1) * L]
-
     pl.semaphore_wait(barrier, len(peers))
 
     along_z = [
@@ -186,23 +201,26 @@
     for each in along_z:
         each.start()
 
+    for each in loads:
+        each.wait()
+    lay_out(row, smp, wgt, cnt, rows, slots, weights)
+    for h in range(H):
+        t2[h * 64 : (h + 1) * 64, :] = tab[:, h * L : (h + 1) * L]
+
     def to_sibling(q):
         block = block_at(jnp.where(q < 2, q + 2, 3 - q))
         return copy(part.at[1 - c, block], from_core.at[q], pc_s.at[q], pc_r.at[q], sibling)
 
-    two_on = [
-        copy(part.at[c, block_at(2), half[0]], from_y.at[0, half[0]], py_s.at[0], py_r.at[0], y_at(1)),
-        copy(part.at[c, block_at(2), half[1]], from_y.at[0, half[1]], py_s.at[1], py_r.at[1], y_at(3)),
-    ]
-    one_on = [
-        copy(part.at[c, block_at(1)], from_y.at[1], py_s.at[2], py_r.at[2], y_at(1)),
-        copy(part.at[c, block_at(3)], from_y.at[2], py_s.at[3], py_r.at[3], y_at(3)),
-    ]
+    two_on = [copy(two_out.at[n], two_in.at[n], py_s.at[n], py_r.at[n], y_at((1, 3)[n])) for n in range(2)]
+    one_on = [copy(one_out.at[n], one_in.at[n], py_s.at[2 + n], py_r.at[2 + n], y_at((1, 3)[n])) for n in range(2)]
+
+    def add(block, n, packed):
+        values = unpack(packed, Z // 2)
+        for j in range(Z // 2):
+            part[c, block, n * (Z // 2) + j] += values[j]
 
     def to_z(d):
-        return copy(
-            part.at[c, y, lax.rem(z + d, Z)], from_z.at[d - 1], pz_s.at[d - 1], pz_r.at[d - 1], z_at(d)
-        )
+        return copy(z_out.at[d - 1], z_in.at[d - 1], pz_s.at[d - 1], pz_r.at[d - 1], z_at(d))
 
     @pl.loop(0, 2 * Y)
     def _(i):
@@ -234,53 +252,55 @@
 
         @pl.when(i == Y)
         def _():
-            for each in two_on:
-                each.start()
-
-        @pl.when(i == 6)
-        def _():
-            for each in along_y:
-                each.wait_recv()
-            for each in further:
-                each.start()
-            to_core(1).start()
-            to_core(2).start()
-            two_on[1].wait_recv()
-            part[c, block_at(3), half[1]] += from_y[0, half[1]]
-            one_on[1].start()
-
-        @pl.when(i == 7)
-        def _():
-            two_on[0].wait_recv()
-            part[c, block_at(1), half[0]] += from_y[0, half[0]]
-            one_on[0].start()
+            for n in range(2):
+                pack(part[c, block_at(2), half[n]], two_out.at[n])
+                two_on[n].start()
+
+    for each in along_y:
+        each.wait_recv()
+    for each in further:
+        each.start()
+    to_core(1).start()
+    to_core(2).start()
+    for n in range(2):
+        two_on[n].wait_recv()
+        add(block_at((1, 3)[n]), n, two_in.at[n])
+        for m in range(2):
+            pack(part[c, block_at((1, 3)[n]), half[m]], one_out.at[n, m])
+        one_on[n].start()
 
     @pl.loop(0, 2 * Y)
     def _(i):
-        k = lax.rem(i, Y)
-        side = jnp.where(i < Y, c, 1 - c)
-        block = block_at(jnp.where(k < 2, k, 5 - k))
-
-        @pl.when(i == 3)
+        k = lax.rem(i, 3)
+        side = jnp.where((i < 3) | (i == 6), c, 1 - c)
+        block = block_at(jnp.where(i >= 6, 2, jnp.where(k == 2, 3, k)))
+
+        for n in range(3):
+
+            @pl.when(i == 3 + n)
+            def _():
+                to_core(n).wait_recv()
+
+        @pl.when(i == 5)
         def _():
             for each in further:
                 each.wait_recv()
             to_core(3).start()
 
-        for n in range(Y):
-
-            @pl.when(i == Y + n)
-            def _():
-                to_core(n).wait_recv()
+        @pl.when(i == 7)
+        def _():
+            to_core(3).wait_recv()
 
         gradient(block * C + side, L, lambda n: gall[side, block, n], rows, slots, weights, a, oh, acc)
 
-        @pl.when(i == 5)
-        def _():
-            for each in one_on:
-                each.wait_recv()
-            part[c, y] += from_y[1] + from_y[2]
+        @pl.when(i == 4)
+        def _():
+            for n in range(2):
+                one_on[n].wait_recv()
+                for m in range(2):
+                    add(y, m, one_in.at[n, m])
             for d in range(1, Z):
+                pack(part[c, y, pl.ds(lax.rem(z + d, Z), 1)], z_out.at[d - 1])
                 to_z(d).start()
 
     for h in range(H):
@@ -296,7 +316,7 @@
         to_z(d).wait_recv()
     total = part[c, y, z]
     for d in range(1, Z):
-        total += from_z[d - 1]
+        total += unpack(z_in.at[d - 1], 1)[0]
     pooled[...] = total
     out = [pltpu.make_async_copy(pooled, pooled_out, store.at[0])]
     out[0].start()
@@ -346,6 +366,7 @@
     _, dim, n_rows = table.shape
     own = grad_pooled.shape[2]
     L = n_rows // H
+    half_rows = (Z // 2) * dim + 16
     dma = pltpu.SemaphoreType.DMA
     anywhere = pl.BlockSpec(memory_space=pl.ANY)
     shapes = (
@@ -370,8 +391,12 @@
             pltpu.VMEM((C, Y, Z, dim, own), BF),
             pltpu.VMEM((C, Y, Z, dim, own), F32),
             pltpu.VMEM((Y, Z, dim, own), F32),
-            pltpu.VMEM((3, Z, dim, own), F32),
-            pltpu.VMEM((Z - 1, dim, own), F32),
+            pltpu.VMEM((2, half_rows, own), jnp.int16),
+            pltpu.VMEM((2, half_rows, own), jnp.int16),
+            pltpu.VMEM((2, 2, half_rows, own), jnp.int16),
+            pltpu.VMEM((2, 2, half_rows, own), jnp.int16),
+            pltpu.VMEM((Z - 1, dim + 16, own), jnp.int16),
+            pltpu.VMEM((Z - 1, dim + 16, own), jnp.int16),
             pltpu.VMEM((X, H, L), F32),
         ]
         + [pltpu.VMEM((dim, n_rows), BF), pltpu.VMEM((1, n_rows), F32)]

time: 41.2 us -> 39.8 us (0.966)
  the two profiles are of different devices: /device:TPU:8 before, /device:TPU:1 now
where the time goes in v3:
time: 39.8 us; the launch traced here: 39.6 us
  Pallas kernels  38.9 us (98%)
  between operations  0.64 us (2%)
    pallas_call x1, Pallas kernels, shards(): pl.pallas_call(kernel, out_shape=shapes, in_specs=[anywhere] * 7, out_spe...  37 us
    pallas_call x1, Pallas kernels, shards(): pl.pallas_call(hand_on, out_shape=shapes, in_specs=[anywhere] * 3, out_sp...  1.91 us

profile of v3, /device:TPU:1, one launch (start us, length us, event | category | flops | bytes accessed | tf_op | source)
XLA Modules:
  0.0 39.6 jit_solution(8398507356021166083)
XLA Ops:
  0.6 37.0 %shard_map.94 = (f32[64,128]{1,0:T(8,128)}, bf16[64,4096]{1,0:T(8,128)(2,1)}, f32[1,4096]{1,0:T(1,128)}) custom-call(bf16[64,4096]{1,0:T(8,128)(2,1)} %bitcast.8, f32[1,4096]{1,0:T(1,128)} %accum_in.1, bf16[64,128]{1,0:T(8,128)(2,1)} %bitcast.12, s32[64,160]{1,0:T(8,128)} %bitcast.9, s32[64,160]{1,0:T(8,128)} %bitcast.10, s32[64,160]{1,0:T(8,128)} %bitcast.11, ...), custom_call_target="tpu_custom_call" | custom-call | tf_op jit(solution)/shard_map/pallas_call | solution.py:377
  37.7 1.9 %shard_map.95 = (f32[64,128]{1,0:T(8,128)}, bf16[64,4096]{1,0:T(8,128)(2,1)}, f32[1,4096]{1,0:T(1,128)}) custom-call(f32[64,128]{1,0:T(8,128)} %get-tuple-element.9.refs_0_, bf16[64,4096]{1,0:T(8,128)(2,1)} %get-tuple-element.10.refs_1_, f32[1,4096]{1,0:T(1,128)} %get-tuple-element.11.refs_2_), custom_call_target="tpu_custom_call" | custom-call | tf_op jit(solution)/shard_map/pallas_call | solution.py:418

commit v4 on v3

--- a/solution.py
+++ b/solution.py
@@ -185,13 +185,17 @@
         return lax.rem(y + d, Y)
 
     half = (pl.ds(0, Z // 2), pl.ds(Z // 2, Z // 2))
-    along_y = [
-        copy(gall.at[c, y], gall.at[c, y], gy_s.at[0], gy_r.at[0], y_at(1)),
-        copy(gall.at[c, y], gall.at[c, y], gy_s.at[1], gy_r.at[1], y_at(3)),
-    ]
+    def along_y(e):
+        at = lax.rem(z + e, Z)
+        return [
+            copy(gall.at[c, y, at], gall.at[c, y, at], gy_s.at[2 + n, e], gy_r.at[2 + n, e], y_at((1, 3)[n]))
+            for n in range(2)
+        ]
+
+    near, far = (0, 1, 2, 6, 7), (3, 4, 5)
     further = [
-        copy(gall.at[c, block_at(3), half[0]], gall.at[c, block_at(3), half[0]], gy_s.at[2], gy_r.at[2], y_at(1)),
-        copy(gall.at[c, block_at(1), half[1]], gall.at[c, block_at(1), half[1]], gy_s.at[3], gy_r.at[3], y_at(3)),
+        copy(gall.at[c, block_at(3), half[0]], gall.at[c, block_at(3), half[0]], gy_s.at[0, 0], gy_r.at[0, 0], y_at(1)),
+        copy(gall.at[c, block_at(1), half[1]], gall.at[c, block_at(1), half[1]], gy_s.at[1, 0], gy_r.at[1, 0], y_at(3)),
     ]
 
     def to_core(k):
@@ -207,11 +211,17 @@
     for h in range(H):
         t2[h * 64 : (h + 1) * 64, :] = tab[:, h * L : (h + 1) * L]
 
+    def order(q):
+        return block_at(jnp.where(q < 2, 2 - q, jnp.where(q == 2, 3, 0)))
+
     def to_sibling(q):
-        block = block_at(jnp.where(q < 2, q + 2, 3 - q))
+        block = order(q)
         return copy(part.at[1 - c, block], from_core.at[q], pc_s.at[q], pc_r.at[q], sibling)
 
-    two_on = [copy(two_out.at[n], two_in.at[n], py_s.at[n], py_r.at[n], y_at((1, 3)[n])) for n in range(2)]
+    two_on = [
+        copy(two_out.at[0], two_in.at[0], py_s.at[0], py_r.at[0], y_at(2)),
+        copy(two_out.at[1], two_in.at[1], py_s.at[1], py_r.at[1], y_at(3)),
+    ]
     one_on = [copy(one_out.at[n], one_in.at[n], py_s.at[2 + n], py_r.at[2 + n], y_at((1, 3)[n])) for n in range(2)]
 
     def add(block, n, packed):
@@ -222,79 +232,98 @@
     def to_z(d):
         return copy(z_out.at[d - 1], z_in.at[d - 1], pz_s.at[d - 1], pz_r.at[d - 1], z_at(d))
 
-    @pl.loop(0, 2 * Y)
-    def _(i):
-        q = lax.rem(i, Y)
-        side = jnp.where(i < Y, 1 - c, c)
-        block = block_at(jnp.where(q < 2, q + 2, 3 - q))
+    def look(q, side, n):
+        block = order(q)
 
         def put(k, value):
             part[side, block, k] = value
 
-        lookup(block * C + side, L, rows, slots, weights, t2, oh, xs, put)
-
-        @pl.when(i < Y)
-        def _():
-            to_sibling(q).start()
-
-        @pl.when(i >= Y)
-        def _():
-            to_sibling(q).wait_recv()
-            part[c, block] += from_core[q]
-
-        @pl.when(i == 3)
-        def _():
-            for each in along_z:
-                each.wait_recv()
-            for each in along_y:
-                each.start()
-            to_core(0).start()
-
-        @pl.when(i == Y)
+        lookup(block * C + side, L, rows, slots, weights, t2, oh.at[n], xs.at[n], put)
+
+    def add_core(q):
+        to_sibling(q).wait_recv()
+        part[c, order(q)] += from_core[q]
+
+    look(0, 1 - c, 0)
+    to_sibling(0).start()
+
+    @pl.loop(0, Y - 1)
+    def _(q):
+        look(q, c, 1)
+        look(q + 1, 1 - c, 0)
+        to_sibling(q + 1).start()
+        add_core(q)
+
+        @pl.when(q == 0)
         def _():
             for n in range(2):
                 pack(part[c, block_at(2), half[n]], two_out.at[n])
                 two_on[n].start()
-
-    for each in along_y:
-        each.wait_recv()
+            for e in near:
+                if e > 0:
+                    along_z[Z - e - 1].wait_recv()
+                for each in along_y(e):
+                    each.start()
+
+        @pl.when(q == 1)
+        def _():
+            for e in far:
+                along_z[Z - e - 1].wait_recv()
+                for each in along_y(e):
+                    each.start()
+            for m in range(2):
+                pack(part[c, block_at(1), half[m]], one_out.at[0, m])
+            one_on[0].start()
+            to_core(0).start()
+
+        @pl.when(q == 2)
+        def _():
+            two_on[1].wait_recv()
+            add(block_at(3), 1, two_in.at[1])
+            for m in range(2):
+                pack(part[c, block_at(3), half[m]], one_out.at[1, m])
+            one_on[1].start()
+
+    look(Y - 1, c, 1)
+    for e in near + far:
+        for each in along_y(e):
+            each.wait_recv()
     for each in further:
         each.start()
     to_core(1).start()
     to_core(2).start()
-    for n in range(2):
-        two_on[n].wait_recv()
-        add(block_at((1, 3)[n]), n, two_in.at[n])
-        for m in range(2):
-            pack(part[c, block_at((1, 3)[n]), half[m]], one_out.at[n, m])
-        one_on[n].start()
-
-    @pl.loop(0, 2 * Y)
+    add_core(Y - 1)
+    to_core(0).wait_recv()
+
+    @pl.loop(0, Y)
     def _(i):
-        k = lax.rem(i, 3)
-        side = jnp.where((i < 3) | (i == 6), c, 1 - c)
-        block = block_at(jnp.where(i >= 6, 2, jnp.where(k == 2, 3, k)))
-
-        for n in range(3):
-
-            @pl.when(i == 3 + n)
-            def _():
-                to_core(n).wait_recv()
-
-        @pl.when(i == 5)
-        def _():
+
+        @pl.when(i == 2)
+        def _():
+            to_core(1).wait_recv()
+            to_core(2).wait_recv()
             for each in further:
                 each.wait_recv()
             to_core(3).start()
 
-        @pl.when(i == 7)
+        @pl.when(i == 3)
         def _():
             to_core(3).wait_recv()
 
-        gradient(block * C + side, L, lambda n: gall[side, block, n], rows, slots, weights, a, oh, acc)
-
-        @pl.when(i == 4)
-        def _():
+        for n in range(2):
+            middle = (i == 1) | (i == 2)
+            side = jnp.where(middle, jnp.where(i == 1, c, 1 - c), c if n == 0 else 1 - c)
+            block = block_at(jnp.where(middle, 1 if n == 0 else 3, jnp.where(i == 0, 0, 2)))
+
+            def grad(k, side=side, block=block):
+                return gall[side, block, k]
+
+            gradient(block * C + side, L, grad, rows, slots, weights, a.at[n], oh.at[n], acc)
+
+        @pl.when(i == 1)
+        def _():
+            two_on[0].wait_recv()
+            add(y, 0, two_in.at[0])
             for n in range(2):
                 one_on[n].wait_recv()
                 for m in range(2):
@@ -337,8 +366,11 @@
     out[1].start()
     out[2].start()
 
-    for each in along_z + along_y + further + two_on + one_on + along_x:
+    for each in along_z + further + two_on + one_on + along_x:
         each.wait_send()
+    for e in range(Z):
+        for each in along_y(e):
+            each.wait_send()
     for q in range(Y):
         to_core(q).wait_send()
         to_sibling(q).wait_send()
@@ -384,9 +416,9 @@
         + [pltpu.VMEM((80, 128), F32)] * 3
         + [
             pltpu.VMEM((64 * H, L), BF),
-            pltpu.VMEM((L, 1280), BF),
-            pltpu.VMEM((64, 2048), BF),
-            pltpu.VMEM((64 * H, 1280), BF),
+            pltpu.VMEM((2, L, 1280), BF),
+            pltpu.VMEM((2, 64, 2048), BF),
+            pltpu.VMEM((2, 64 * H, 1280), BF),
             pltpu.VMEM((64 * H, L), F32),
             pltpu.VMEM((C, Y, Z, dim, own), BF),
             pltpu.VMEM((C, Y, Z, dim, own), F32),
@@ -402,7 +434,9 @@
         + [pltpu.VMEM((dim, n_rows), BF), pltpu.VMEM((1, n_rows), F32)]
         + [pltpu.VMEM(sample_slot.shape[2:], jnp.int32)] * 3
         + [pltpu.VMEM(send_count.shape[1:], jnp.int32)]
-        + [dma((n,)) for n in (7, 7, 7, 4, 4, 4, 4, 4, 4, 4, 4, 7, 7, 3, 3)],
+        + [dma((n,)) for n in (7, 7, 7)]
+        + [dma((4, Z)), dma((4, Z))]
+        + [dma((n,)) for n in (4, 4, 4, 4, 4, 4, 7, 7, 3, 3)],
         compiler_params=pltpu.CompilerParams(
             collective_id=0, has_side_effects=True, vmem_limit_bytes=64 << 20
         ),

time: 39.8 us -> 37 us (0.930)
  the two profiles are of different devices: /device:TPU:1 before, /device:TPU:8 now
where the time goes in v4:
time: 37 us; the launch traced here: 36.8 us
  Pallas kernels  36.2 us (98%)
  between operations  0.64 us (2%)
    pallas_call x1, Pallas kernels, shards(): pl.pallas_call(kernel, out_shape=shapes, in_specs=[anywhere] * 7, out_spe...  34.3 us
    pallas_call x1, Pallas kernels, shards(): pl.pallas_call(hand_on, out_shape=shapes, in_specs=[anywhere] * 3, out_sp...  1.91 us

profile of v4, /device:TPU:8, one launch (start us, length us, event | category | flops | bytes accessed | tf_op | source)
XLA Modules:
  0.0 36.8 jit_solution(17327656120759264321)
XLA Ops:
  0.6 34.3 %shard_map.94 = (f32[64,128]{1,0:T(8,128)}, bf16[64,4096]{1,0:T(8,128)(2,1)}, f32[1,4096]{1,0:T(1,128)}) custom-call(bf16[64,4096]{1,0:T(8,128)(2,1)} %bitcast.8, f32[1,4096]{1,0:T(1,128)} %accum_in.1, bf16[64,128]{1,0:T(8,128)(2,1)} %bitcast.12, s32[64,160]{1,0:T(8,128)} %bitcast.9, s32[64,160]{1,0:T(8,128)} %bitcast.10, s32[64,160]{1,0:T(8,128)} %bitcast.11, ...), custom_call_target="tpu_custom_call" | custom-call | tf_op jit(solution)/shard_map/pallas_call | solution.py:409
  34.9 1.9 %shard_map.95 = (f32[64,128]{1,0:T(8,128)}, bf16[64,4096]{1,0:T(8,128)(2,1)}, f32[1,4096]{1,0:T(1,128)}) custom-call(f32[64,128]{1,0:T(8,128)} %get-tuple-element.9.refs_0_, bf16[64,4096]{1,0:T(8,128)(2,1)} %get-tuple-element.10.refs_1_, f32[1,4096]{1,0:T(1,128)} %get-tuple-element.11.refs_2_), custom_call_target="tpu_custom_call" | custom-call | tf_op jit(solution)/shard_map/pallas_call | solution.py:452

commit v5 on v4

--- a/solution.py
+++ b/solution.py
@@ -144,10 +144,13 @@
     L = tab.shape[1] // H
     pairs = ((cnt_in, cnt), (wgt_in, wgt), (row_in, row), (smp_in, smp), (tab_in, tab), (accum_in, accum))
     loads = [pltpu.make_async_copy(src, dst, load.at[i]) for i, (src, dst) in enumerate(pairs)]
+    r, x = lax.axis_index("rows"), lax.axis_index("dims")
+    z, y, c = r // (Y * C), lax.rem(r // C, Y), lax.rem(r, C)
+
+    own_grad = pltpu.make_async_copy(g, gall.at[c, y, z], load.at[len(pairs)])
+    own_grad.start()
     for each in loads:
         each.start()
-    r, x = lax.axis_index("rows"), lax.axis_index("dims")
-    z, y, c = r // (Y * C), lax.rem(r // C, Y), lax.rem(r, C)
 
     def z_at(d):
         return (lax.rem(z + d, Z) * (Y * C) + y * C + c, x)
@@ -171,8 +174,6 @@
     for to in peers:
         pl.semaphore_signal(barrier, inc=1, device_id=to, device_id_type=MESH)
 
-    own_grad = pltpu.make_async_copy(g, gall.at[c, y, z], load.at[len(pairs)])
-    own_grad.start()
     acc[...] = jnp.zeros_like(acc)
     own_grad.wait()
     pl.semaphore_wait(barrier, len(peers))
@@ -188,15 +189,16 @@
     def along_y(e):
         at = lax.rem(z + e, Z)
         return [
-            copy(gall.at[c, y, at], gall.at[c, y, at], gy_s.at[2 + n, e], gy_r.at[2 + n, e], y_at((1, 3)[n]))
+            copy(gall.at[c, y, at], gall.at[c, y, at], gy_s.at[1 + n, e], gy_r.at[1 + n, e], y_at((1, 3)[n]))
             for n in range(2)
         ]
 
     near, far = (0, 1, 2, 6, 7), (3, 4, 5)
-    further = [
-        copy(gall.at[c, block_at(3), half[0]], gall.at[c, block_at(3), half[0]], gy_s.at[0, 0], gy_r.at[0, 0], y_at(1)),
-        copy(gall.at[c, block_at(1), half[1]], gall.at[c, block_at(1), half[1]], gy_s.at[1, 0], gy_r.at[1, 0], y_at(3)),
-    ]
+    def further(e):
+        at = lax.rem(z + e, Z)
+        up = e in (0, 1, 6, 3)
+        block = block_at(3 if up else 1)
+        return copy(gall.at[c, block, at], gall.at[c, block, at], gy_s.at[0, e], gy_r.at[0, e], y_at(1 if up else 3))
 
     def to_core(k):
         block = block_at((0, 1, 3, 2)[k])
@@ -256,14 +258,14 @@
 
         @pl.when(q == 0)
         def _():
-            for n in range(2):
-                pack(part[c, block_at(2), half[n]], two_out.at[n])
-                two_on[n].start()
             for e in near:
                 if e > 0:
                     along_z[Z - e - 1].wait_recv()
                 for each in along_y(e):
                     each.start()
+            for n in (1, 0):
+                pack(part[c, block_at(2), half[n]], two_out.at[n])
+                two_on[n].start()
 
         @pl.when(q == 1)
         def _():
@@ -278,47 +280,51 @@
 
         @pl.when(q == 2)
         def _():
+            for e in near:
+                for each in along_y(e):
+                    each.wait_recv()
+                further(e).start()
             two_on[1].wait_recv()
             add(block_at(3), 1, two_in.at[1])
             for m in range(2):
                 pack(part[c, block_at(3), half[m]], one_out.at[1, m])
             one_on[1].start()
 
+    def grad_of(side, d, n):
+        block = block_at(d)
+
+        def grad(k):
+            return gall[side, block, k]
+
+        gradient(block * C + side, L, grad, rows, slots, weights, a.at[n], oh.at[n], acc)
+
     look(Y - 1, c, 1)
-    for e in near + far:
+    grad_of(c, 0, 0)
+    for e in far:
         for each in along_y(e):
             each.wait_recv()
-    for each in further:
-        each.start()
+        further(e).start()
     to_core(1).start()
     to_core(2).start()
     add_core(Y - 1)
     to_core(0).wait_recv()
 
-    @pl.loop(0, Y)
+    @pl.loop(0, Y - 1)
     def _(i):
 
+        @pl.when(i == 1)
+        def _():
+            to_core(1).wait_recv()
+
         @pl.when(i == 2)
         def _():
-            to_core(1).wait_recv()
+            for e in range(Z):
+                further(e).wait_recv()
+            to_core(3).start()
             to_core(2).wait_recv()
-            for each in further:
-                each.wait_recv()
-            to_core(3).start()
-
-        @pl.when(i == 3)
-        def _():
-            to_core(3).wait_recv()
-
-        for n in range(2):
-            middle = (i == 1) | (i == 2)
-            side = jnp.where(middle, jnp.where(i == 1, c, 1 - c), c if n == 0 else 1 - c)
-            block = block_at(jnp.where(middle, 1 if n == 0 else 3, jnp.where(i == 0, 0, 2)))
-
-            def grad(k, side=side, block=block):
-                return gall[side, block, k]
-
-            gradient(block * C + side, L, grad, rows, slots, weights, a.at[n], oh.at[n], acc)
+
+        grad_of(jnp.where(i == 1, c, 1 - c), jnp.where(i == 0, 0, 3), 0)
+        grad_of(jnp.where(i == 1, 1 - c, c), jnp.where(i == 2, 2, 1), 1)
 
         @pl.when(i == 1)
         def _():
@@ -332,6 +338,9 @@
                 pack(part[c, y, pl.ds(lax.rem(z + d, Z), 1)], z_out.at[d - 1])
                 to_z(d).start()
 
+    to_core(3).wait_recv()
+    grad_of(1 - c, 2, 0)
+
     for h in range(H):
         v = acc[h * 64 : (h + 1) * 64, :]
         squares[x, h : h + 1, :] = jnp.sum(v * v, axis=0, keepdims=True)
@@ -359,16 +368,17 @@
         new_accum[:, cols] = new
         moved = acc[h * 64 : (h + 1) * 64, :] * (STEP * lax.rsqrt(new))
         new_tab[:, cols] = (tab[:, cols].astype(F32) - moved).astype(BF)
-    out += [
-        pltpu.make_async_copy(new_tab, new_tab_out, store.at[1]),
-        pltpu.make_async_copy(new_accum, new_accum_out, store.at[2]),
-    ]
-    out[1].start()
-    out[2].start()
-
-    for each in along_z + further + two_on + one_on + along_x:
+        if h % 2 == 1:
+            cols = pl.ds((h - 1) * L, 2 * L)
+            out.append(pltpu.make_async_copy(new_tab.at[:, cols], new_tab_out.at[:, cols], store.at[2 + h // 2]))
+            out[-1].start()
+    out.append(pltpu.make_async_copy(new_accum, new_accum_out, store.at[1]))
+    out[-1].start()
+
+    for each in along_z + two_on + one_on + along_x:
         each.wait_send()
     for e in range(Z):
+        further(e).wait_send()
         for each in along_y(e):
             each.wait_send()
     for q in range(Y):
@@ -383,13 +393,15 @@
 def hand_on(*refs):
     n = (len(refs) - 2) // 3
     src, dst, held, come, go = refs[:n], refs[n : 2 * n], refs[2 * n : 3 * n], refs[-2], refs[-1]
-    loads = [pltpu.make_async_copy(src[i], held[i], come.at[i]) for i in range(n)]
-    stores = [pltpu.make_async_copy(held[i], dst[i], go.at[i]) for i in range(n)]
+    pieces = [(src[1].at[rows], held[1].at[rows], dst[1].at[rows]) for rows in [pl.ds(16 * k, 16) for k in range(4)]]
+    pieces += [(src[i], held[i], dst[i]) for i in (0, 2)]
+    loads = [pltpu.make_async_copy(p[0], p[1], come.at[i]) for i, p in enumerate(pieces)]
+    stores = [pltpu.make_async_copy(p[1], p[2], go.at[i]) for i, p in enumerate(pieces)]
     for each in loads:
         each.start()
-    for i in range(n):
-        loads[i].wait()
-        stores[i].start()
+    for load, store in zip(loads, stores):
+        load.wait()
+        store.start()
     for each in stores:
         each.wait()
 
@@ -412,7 +424,7 @@
         in_specs=[anywhere] * 7,
         out_specs=(anywhere,) * 3,
         scratch_shapes=[pltpu.VMEM(each.shape, each.dtype) for each in shapes]
-        + [dma((3,))]
+        + [dma((2 + H // 2,))]
         + [pltpu.VMEM((80, 128), F32)] * 3
         + [
             pltpu.VMEM((64 * H, L), BF),
@@ -435,7 +447,7 @@
         + [pltpu.VMEM(sample_slot.shape[2:], jnp.int32)] * 3
         + [pltpu.VMEM(send_count.shape[1:], jnp.int32)]
         + [dma((n,)) for n in (7, 7, 7)]
-        + [dma((4, Z)), dma((4, Z))]
+        + [dma((3, Z)), dma((3, Z))]
         + [dma((n,)) for n in (4, 4, 4, 4, 4, 4, 7, 7, 3, 3)],
         compiler_params=pltpu.CompilerParams(
             collective_id=0, has_side_effects=True, vmem_limit_bytes=64 << 20
@@ -454,7 +466,7 @@
         out_shape=shapes,
         in_specs=[anywhere] * 3,
         out_specs=(anywhere,) * 3,
-        scratch_shapes=[pltpu.VMEM(each.shape, each.dtype) for each in shapes] + [dma((3,)), dma((3,))],
+        scratch_shapes=[pltpu.VMEM(each.shape, each.dtype) for each in shapes] + [dma((6,)), dma((6,))],
         compiler_params=pltpu.CompilerParams(vmem_limit_bytes=64 << 20),
     )(*results)
     return pooled[None], new_table[None], new_accum

time: 37 us -> 36.5 us (0.986)
  Pallas kernels: 36.2 us -> 35.7 us
    pallas_call x1, Pallas kernels: 34.3 us -> 33.9 us  [shards(): pl.pallas_call(kernel, out_shape=shapes, in_specs=[anywhere] * 7, out_spe...]
where the time goes in v5:
time: 36.5 us; the launch traced here: 36.4 us
  Pallas kernels  35.7 us (98%)
  between operations  0.64 us (2%)
    pallas_call x1, Pallas kernels, shards(): pl.pallas_call(kernel, out_shape=shapes, in_specs=[anywhere] * 7, out_spe...  33.9 us
    pallas_call x1, Pallas kernels, shards(): pl.pallas_call(hand_on, out_shape=shapes, in_specs=[anywhere] * 3, out_sp...  1.86 us

profile of v5, /device:TPU:8, one launch (start us, length us, event | category | flops | bytes accessed | tf_op | source)
XLA Modules:
  0.0 36.4 jit_solution(6598956504222365976)
XLA Ops:
  0.6 33.9 %shard_map.94 = (f32[64,128]{1,0:T(8,128)}, bf16[64,4096]{1,0:T(8,128)(2,1)}, f32[1,4096]{1,0:T(1,128)}) custom-call(bf16[64,4096]{1,0:T(8,128)(2,1)} %bitcast.8, f32[1,4096]{1,0:T(1,128)} %accum_in.1, bf16[64,128]{1,0:T(8,128)(2,1)} %bitcast.12, s32[64,160]{1,0:T(8,128)} %bitcast.9, s32[64,160]{1,0:T(8,128)} %bitcast.10, s32[64,160]{1,0:T(8,128)} %bitcast.11, ...), custom_call_target="tpu_custom_call" | custom-call | tf_op jit(solution)/shard_map/pallas_call | solution.py:421
  34.5 1.9 %shard_map.95 = (f32[64,128]{1,0:T(8,128)}, bf16[64,4096]{1,0:T(8,128)(2,1)}, f32[1,4096]{1,0:T(1,128)}) custom-call(f32[64,128]{1,0:T(8,128)} %get-tuple-element.9.refs_0_, bf16[64,4096]{1,0:T(8,128)(2,1)} %get-tuple-element.10.refs_1_, f32[1,4096]{1,0:T(1,128)} %get-tuple-element.11.refs_2_), custom_call_target="tpu_custom_call" | custom-call | tf_op jit(solution)/shard_map/pallas_call | solution.py:464

commit v6 on v5

--- a/solution.py
+++ b/solution.py
@@ -193,7 +193,7 @@
             for n in range(2)
         ]
 
-    near, far = (0, 1, 2, 6, 7), (3, 4, 5)
+    near, far = (0, 1, 7), (2, 3, 4, 5, 6)
     def further(e):
         at = lax.rem(z + e, Z)
         up = e in (0, 1, 6, 3)

time: 36.5 us -> 36.2 us (level); the launches traced: 36.4 us -> 35.6 us
  Pallas kernels: 35.7 us -> 35 us
    pallas_call x1, Pallas kernels: 33.9 us -> 33.1 us  [shards(): pl.pallas_call(kernel, out_shape=shapes, in_specs=[anywhere] * 7, out_spe...]
where the time goes in v6:
time: 36.2 us; the launch traced here: 35.6 us
  Pallas kernels  35 us (97%)
  between operations  0.64 us (2%)
    pallas_call x1, Pallas kernels, shards(): pl.pallas_call(kernel, out_shape=shapes, in_specs=[anywhere] * 7, out_spe...  33.1 us
    pallas_call x1, Pallas kernels, shards(): pl.pallas_call(hand_on, out_shape=shapes, in_specs=[anywhere] * 3, out_sp...  1.86 us

profile of v6, /device:TPU:8, one launch (start us, length us, event | category | flops | bytes accessed | tf_op | source)
XLA Modules:
  0.0 35.6 jit_solution(793033434558234599)
XLA Ops:
  0.6 33.1 %shard_map.94 = (f32[64,128]{1,0:T(8,128)}, bf16[64,4096]{1,0:T(8,128)(2,1)}, f32[1,4096]{1,0:T(1,128)}) custom-call(bf16[64,4096]{1,0:T(8,128)(2,1)} %bitcast.8, f32[1,4096]{1,0:T(1,128)} %accum_in.1, bf16[64,128]{1,0:T(8,128)(2,1)} %bitcast.12, s32[64,160]{1,0:T(8,128)} %bitcast.9, s32[64,160]{1,0:T(8,128)} %bitcast.10, s32[64,160]{1,0:T(8,128)} %bitcast.11, ...), custom_call_target="tpu_custom_call" | custom-call | tf_op jit(solution)/shard_map/pallas_call | solution.py:421
  33.8 1.9 %shard_map.95 = (f32[64,128]{1,0:T(8,128)}, bf16[64,4096]{1,0:T(8,128)(2,1)}, f32[1,4096]{1,0:T(1,128)}) custom-call(f32[64,128]{1,0:T(8,128)} %get-tuple-element.9.refs_0_, bf16[64,4096]{1,0:T(8,128)(2,1)} %get-tuple-element.10.refs_1_, f32[1,4096]{1,0:T(1,128)} %get-tuple-element.11.refs_2_), custom_call_target="tpu_custom_call" | custom-call | tf_op jit(solution)/shard_map/pallas_call | solution.py:464

commit v7 on v6

--- a/solution.py
+++ b/solution.py
@@ -175,11 +175,10 @@
         pl.semaphore_signal(barrier, inc=1, device_id=to, device_id_type=MESH)
 
     acc[...] = jnp.zeros_like(acc)
-    own_grad.wait()
     pl.semaphore_wait(barrier, len(peers))
 
     along_z = [
-        copy(gall.at[c, y, z], gall.at[c, y, z], gz_s.at[d - 1], gz_r.at[d - 1], z_at(d)) for d in range(1, Z)
+        copy(g, gall.at[c, y, z], gz_s.at[d - 1], gz_r.at[d - 1], z_at(d)) for d in range(1, Z)
     ]
 
     def block_at(d):
@@ -207,7 +206,7 @@
     for each in along_z:
         each.start()
 
-    for each in loads:
+    for each in [own_grad] + loads:
         each.wait()
     lay_out(row, smp, wgt, cnt, rows, slots, weights)
     for h in range(H):

time: 36.2 us -> 36.2 us (level)
  no operation moved by 1% of the time
where the time goes in v7:
time: 36.2 us; the launch traced here: 35.7 us
  Pallas kernels  35 us (97%)
  between operations  0.64 us (2%)
    pallas_call x1, Pallas kernels, shards(): pl.pallas_call(kernel, out_shape=shapes, in_specs=[anywhere] * 7, out_spe...  33.2 us
    pallas_call x1, Pallas kernels, shards(): pl.pallas_call(hand_on, out_shape=shapes, in_specs=[anywhere] * 3, out_sp...  1.86 us

profile of v7, /device:TPU:8, one launch (start us, length us, event | category | flops | bytes accessed | tf_op | source)
XLA Modules:
  0.0 35.7 jit_solution(17404802898195914881)
XLA Ops:
  0.6 33.2 %shard_map.94 = (f32[64,128]{1,0:T(8,128)}, bf16[64,4096]{1,0:T(8,128)(2,1)}, f32[1,4096]{1,0:T(1,128)}) custom-call(bf16[64,4096]{1,0:T(8,128)(2,1)} %bitcast.8, f32[1,4096]{1,0:T(1,128)} %accum_in.1, bf16[64,128]{1,0:T(8,128)(2,1)} %bitcast.12, s32[64,160]{1,0:T(8,128)} %bitcast.9, s32[64,160]{1,0:T(8,128)} %bitcast.10, s32[64,160]{1,0:T(8,128)} %bitcast.11, ...), custom_call_target="tpu_custom_call" | custom-call | tf_op jit(solution)/shard_map/pallas_call | solution.py:420
  33.8 1.9 %shard_map.95 = (f32[64,128]{1,0:T(8,128)}, bf16[64,4096]{1,0:T(8,128)(2,1)}, f32[1,4096]{1,0:T(1,128)}) custom-call(f32[64,128]{1,0:T(8,128)} %get-tuple-element.9.refs_0_, bf16[64,4096]{1,0:T(8,128)(2,1)} %get-tuple-element.10.refs_1_, f32[1,4096]{1,0:T(1,128)} %get-tuple-element.11.refs_2_), custom_call_target="tpu_custom_call" | custom-call | tf_op jit(solution)/shard_map/pallas_call | solution.py:463
